TPU v7x, 128 devices: a whole 4x4x4 slice. The times are simulated.
128 devices in a mesh: row: 16 (over x, z_hi, core), col: 8 (over z_lo, y).
Axes of the slice: x: 4, y: 4, z: 4 (z_hi: 2, z_lo: 2; z = z_hi * 2 + z_lo), core: 2. Of those that a mesh axis runs over, the one named last changes fastest.
Arguments:
- hidden_acts: bfloat16 [1, 512, 28672], P(None, 'col', 'row'), may hold values from -6 to 6
- out_grads: bfloat16 [1, 512, 8192], P(None, 'row', 'col'), may hold values from -0.119628906 to 0.119628906
- second_moment: float32 [28672, 8192], P('row', 'col'), may hold values from 0.01 to 1
- sign_flips: bfloat16 [28672, 8192], P('row', 'col'), may hold values from -1 to 1, as said below
- kept_rows: int32 [1, 16384], replicated, may hold values from 0 to 32767
- kept_cols: int32 [1, 16384], replicated, may hold values from 0 to 8191
Outputs:
- sketch: float32 [1, 16384], P(None, ('row', 'col'))
Inputs may be any that keep to these rules, and one draw needn't show every extreme that they name: `sign_flips`: every entry is +1 or -1.
All inputs are finite; a program needn't handle non-finite values.
Results may differ from a plain program's by a relative error of at most 0.0003.
Values may be sent and summed in bfloat16 or wider, within the bound.
No kernel may reach another device: no remote copies, remote signals or barrier semaphores. Data moves between devices by JAX's collectives and lax.ppermute only.
A program may use at most 128 MiB of HBM per device.

v0:
```python
import math

import jax
import jax.numpy as jnp
from jax import lax
from jax.sharding import PartitionSpec as P

D = 8192
GROUP = 1792
GROUP_PAD = 2048
ROWS_PAD = 32768


EPSILON = 1e-08


def parity(values, bit_count):
    ones_count = jnp.zeros_like(values)
    for bit_number in range(bit_count):
        ones_count = ones_count + (values >> bit_number & 1)
    return ones_count & 1


def sylvester(matrix_order):
    ordinal = jnp.arange(matrix_order, dtype=jnp.int32)
    bits_set = parity(ordinal[:, None] & ordinal[None, :], matrix_order.bit_length())
    return (1 - 2 * bits_set).astype(jnp.float32)


def rows_transform(values_in):
    examples, length, width = values_in.shape
    inner_len = min(length, 128)
    outer_len = length // inner_len
    shaped = values_in.reshape(examples, outer_len, inner_len, width)
    shaped = jnp.einsum(
        "ij,eajm->eaim", sylvester(inner_len), shaped, precision=lax.Precision.HIGHEST
    )
    shaped = jnp.einsum(
        "ij,ejbm->eibm", sylvester(outer_len), shaped, precision=lax.Precision.HIGHEST
    )
    return shaped.reshape(examples, length, width)


def cols_transform(values_in):
    examples, height, length = values_in.shape
    inner_len = min(length, 128)
    outer_len = length // inner_len
    shaped = values_in.reshape(examples, height, outer_len, inner_len)
    shaped = jnp.einsum(
        "erab,jb->eraj", shaped, sylvester(inner_len), precision=lax.Precision.HIGHEST
    )
    shaped = jnp.einsum(
        "erab,ia->erib", shaped, sylvester(outer_len), precision=lax.Precision.HIGHEST
    )
    return shaped.reshape(examples, height, length)


def shards(hidden_acts, out_grads, second_moment, sign_flips, kept_rows, kept_cols):
    acts_all = lax.all_gather(hidden_acts, "col", axis=1, tiled=True)
    grads_all = lax.all_gather(out_grads, "row", axis=1, tiled=True)
    gradient = jnp.einsum("etf,etd->efd", acts_all, grads_all, preferred_element_type=jnp.float32)
    examples, local_rows, local_cols = gradient.shape
    groups = local_rows // GROUP
    norm_scale = 1.0 / math.sqrt(ROWS_PAD * D)
    factor = sign_flips.astype(jnp.float32) / (jnp.sqrt(second_moment) + EPSILON) * norm_scale
    scaled = gradient * factor[None]
    padded = jnp.pad(
        scaled.reshape(examples, groups, GROUP, local_cols),
        ((0, 0), (0, 0), (0, GROUP_PAD - GROUP), (0, 0)),
    )
    pad_rows = groups * GROUP_PAD
    padded = padded.reshape(examples, pad_rows, local_cols)
    transformed = cols_transform(rows_transform(padded))
    row_dev = lax.axis_size("row")
    col_dev = lax.axis_size("col")
    my_row = lax.axis_index("row")
    my_col = lax.axis_index("col")
    block_row = kept_rows // pad_rows
    offset_row = kept_rows % pad_rows
    block_col = kept_cols // local_cols
    offset_col = kept_cols % local_cols
    exchanged = lax.all_to_all(
        lax.all_to_all(transformed, "row", split_axis=1, concat_axis=1, tiled=True),
        "col",
        split_axis=2,
        concat_axis=2,
        tiled=True,
    )
    share_rows = pad_rows // row_dev
    share_cols = local_cols // col_dev
    shaped = exchanged.reshape(examples, row_dev, share_rows, col_dev, share_cols)
    shaped = jnp.einsum(
        "as,esutv->eautv", sylvester(row_dev), shaped, precision=lax.Precision.HIGHEST
    )
    shaped = jnp.einsum(
        "bt,eautv->eaubv", sylvester(col_dev), shaped, precision=lax.Precision.HIGHEST
    )
    is_here = (offset_row // share_rows == my_row) & (offset_col // share_cols == my_col)
    position = (
        (block_row * share_rows + offset_row % share_rows) * col_dev + block_col
    ) * share_cols + offset_col % share_cols
    picked = jnp.take_along_axis(shaped.reshape(examples, -1), position, axis=1)
    contribution = jnp.where(is_here, picked, jnp.zeros_like(picked))
    return lax.psum_scatter(contribution, ("row", "col"), scatter_dimension=1, tiled=True)


def solution(mesh):
    placed = (
        P(None, "col", "row"),
        P(None, "row", "col"),
        P("row", "col"),
        P("row", "col"),
        P(),
        P(),
    )
    return jax.shard_map(
        shards, mesh=mesh, in_specs=placed, out_specs=P(None, ("row", "col")), check_vma=False
    )
```

profile of v0, /device:TPU:0, one launch (start us, length us, event | category | flops | bytes accessed | tf_op | source)
XLA Modules:
  0.0 1321.4 jit_solution(13595413336846867890)
XLA Ops:
  6.5 0.0 all-gather.5.cloned.1.call-start
  6.5 0.7 all-gather.5.cloned.1.call-update
  7.3 0.0 all-gather.3.cloned.1.call-start
  7.3 0.7 all-gather.3.cloned.1.call-update
  8.0 49.3 %all-gather.5.cloned.1.call-done = bf16[1,512,1024]{2,1,0:T(8,128)(2,1)} async-done(((bf16[1,32,1024]{2,1,0:T(8,128)(2,1)}), bf16[1,512,1024]{2,1,0:T(8,128)(2,1)}) %all-gather.5.cloned.1.call-update) | async-done | bytes 1048592 | tf_op jit(solution)/shard_map/all_gather | solution.py:60
  57.3 41.3 %all-gather.3.cloned.1.call-done = bf16[1,512,1792]{2,1,0:T(8,128)(2,1)} async-done(((bf16[1,64,1792]{2,1,0:T(8,128)(2,1)}), bf16[1,512,1792]{2,1,0:T(8,128)(2,1)}) %all-gather.3.cloned.1.call-update) | async-done | bytes 1835024 | tf_op jit(solution)/shard_map/all_gather | solution.py:59
  98.6 9.4 multiply_bitcast_fusion
  108.0 1.5 pad.4
  109.5 15.9 %convolution_bitcast_fusion.2 = f32[16,128,1024]{1,2,0:T(8,128)} fusion(f32[16,128,1024]{2,1,0:T(8,128)S(1)} %bitcast.71), kind=kOutput, calls=%fused_computation.6 | convolution fusion | flops 3221684224 | bytes 16777216 | tf_op jit(solution)/shard_map/ij,eajm->eaim/dot_general | solution.py:35
  125.4 8.8 copy.16
  134.2 13.8 %convolution_bitcast_fusion.1 = f32[1,16,128,1024]{3,1,2,0:T(8,128)S(1)} fusion(f32[16,128,1024]{2,0,1:T(8,128)} %copy.16), kind=kOutput, calls=%fused_computation.5 | convolution fusion | flops 402658048 | bytes 16777216 | tf_op jit(solution)/shard_map/ij,ejbm->eibm/dot_general | solution.py:38
  148.0 4.9 copy.17
  152.8 2.1 copy.30
  154.9 7.6 fusion.6
  162.6 8.8 fusion.16
  171.3 103.2 %all_to_all.10 = f32[1,2048,1024]{2,0,1:T(1,128)} all-to-all(f32[1,2048,1024]{2,0,1:T(1,128)S(1)} %bitcast.75), channel_id=1, replica_groups=mesh['row'=16,'col'=8] {'row'}, dimensions={1} | all-to-all | bytes 16777216 | tf_op jit(solution)/shard_map/all_to_all | solution.py:83
  274.5 29.6 %copy.19 = f32[1,2048,1024]{1,0,2:T(1,128)} copy(f32[1,2048,1024]{2,0,1:T(1,128)} %all_to_all.10) | data formatting | bytes 16777216 | tf_op jit(solution)/shard_map/all_to_all | solution.py:83
  304.1 0.0 copy-start
  304.1 0.0 copy-start.1
  304.1 5.1 all-to-all-start.1
  309.2 0.0 reduce-scatter.4.cloned.1.call-start
  309.2 0.0 copy-done
  309.2 0.0 copy-done.1
  309.2 1.4 compare_select_fusion
  310.7 92.5 %all-to-all-done.1 = f32[1,2048,1024]{1,0,2:T(1,128)} async-done(((f32[1,2048,1024]{1,0,2:T(1,128)}), f32[1,2048,1024]{1,0,2:T(1,128)}, u32[]{:S(2)}, u32[]{:S(2)}) %all-to-all-start.1) | async-done | bytes 8388640 | tf_op jit(solution)/shard_map/all_to_all | solution.py:82
  403.2 9.4 copy.21
  412.5 10.1 convolution_bitcast_fusion
  422.7 12.1 fusion
  434.8 192.2 %gather_fusion = f32[16384]{0:T(1024)S(1)} fusion(f32[2097152]{0:T(1024)} %bitcast.70, s32[16384]{0:T(1024)S(1)} %broadcast_clamp_fusion), kind=kCustom, calls=%fused_computation | custom fusion | bytes 196608 | tf_op jit(solution)/shard_map/jit(take_along_axis)/gather | solution.py:102
  627.0 1.1 and_select_fusion.5
  628.1 4.9 copy.28
  633.0 0.0 reduce-scatter.4.cloned.1.call-update
  633.0 680.0 %reduce-scatter.4.cloned.1.call-done = f32[128,1]{1,0:T(8,128)} async-done(((f32[16384,1]{1,0:T(8,128)}), f32[128,1]{1,0:T(8,128)}) %reduce-scatter.4.cloned.1.call-update) | async-done | bytes 528
  1313.0 1.4 copy.29
  (1 shorter events, 0.0 us)
Async XLA Ops:
  6.5 50.8 %all-gather.5.cloned.1.call-start = ((), (), s32[]{:S(2)}) async-start(), calls=%async_computation.4 | async-start | bytes 1114112 | tf_op jit(solution)/shard_map/all_gather | solution.py:60
  7.3 91.4 %all-gather.3.cloned.1.call-start = ((), (), s32[]{:S(2)}) async-start(), calls=%async_computation.3 | async-start | bytes 2064384 | tf_op jit(solution)/shard_map/all_gather | solution.py:59
  304.1 5.1 copy-start
  304.1 5.2 copy-start.1
  304.1 99.1 %all-to-all-start.1 = ((f32[1,2048,1024]{1,0,2:T(1,128)}), f32[1,2048,1024]{1,0,2:T(1,128)}, u32[]{:S(2)}, u32[]{:S(2)}) async-start(f32[1,2048,1024]{1,0,2:T(1,128)} %copy.19), calls=%async_computation.1 | async-start | bytes 16777216 | tf_op jit(solution)/shard_map/all_to_all | solution.py:82
  309.2 1003.9 %reduce-scatter.4.cloned.1.call-start = ((), (), s32[]{:S(2)}) async-start(), calls=%async_computation.5 | async-start | bytes 8454144
Sparse Core Ops, SparseCore 0:
  9.8 47.5 all-gather.4
  59.0 39.6 all-gather.2
  633.1 679.8 reduce-scatter.3
where the time goes:
time: 1330 us; the launch traced here: 1320 us
  waiting for transfers between devices  865 us (65%)
  local copies, waits for them, and re-layouts  255 us (19%)
  blocking collectives  103 us (8%)
  matrix products  77.7 us (6%)
  between operations  13.7 us (1%)
    unnamed x4, waiting for transfers between devices  681 us
    gather x1, local copies, waits for them, and re-layouts, shards(): picked = jnp.take_along_axis(shaped.reshape(examples, -1), position, axis=1)  192 us
    all_to_all x1, blocking collectives, shards(): lax.all_to_all(transformed, 'row', split_axis=1, concat_axis=1, tiled=True)  103 us
    all_to_all x1, waiting for transfers between devices, shards(): lax.all_to_all(lax.all_to_all(transformed, 'row', split_axis=1, concat_ax...  92.5 us
    all_gather x1, waiting for transfers between devices, shards(): grads_all = lax.all_gather(out_grads, 'row', axis=1, tiled=True)  49.3 us
    all_gather x1, waiting for transfers between devices, shards(): acts_all = lax.all_gather(hidden_acts, 'col', axis=1, tiled=True)  41.3 us
    all_to_all x1, local copies, waits for them, and re-layouts, shards(): lax.all_to_all(transformed, 'row', split_axis=1, concat_axis=1, tiled=True)  29.6 us
  transfers between devices with their start and end apart: 4, of which 4 were waited for; matrix products, arithmetic and copies ran while one was open for 0% of the time, Pallas kernels for 0%

commit v1 on v0

v1 whole, which is shorter than its diff:
```python
import functools
import math

import jax
import jax.numpy as jnp
from jax import lax
from jax.experimental import pallas as pl
from jax.experimental.pallas import tpu as pltpu
from jax.sharding import PartitionSpec as P

D = 8192
GROUP = 1792
GROUP_PAD = 2048
ROWS_PAD = 32768
EPSILON = 1e-08

LANES = 128
SUBLANES = 8
TILE = 256


def parity(values):
    for shift in (8, 4, 2, 1):
        values = values ^ (values >> shift)
    return values & 1


def sylvester(order):
    i = lax.broadcasted_iota(jnp.int32, (order, order), 0)
    j = lax.broadcasted_iota(jnp.int32, (order, order), 1)
    return (1 - 2 * parity(i & j)).astype(jnp.float32).astype(jnp.bfloat16)


def halves(x):
    high = x.astype(jnp.bfloat16)
    low = (x - high.astype(jnp.float32)).astype(jnp.bfloat16)
    return high, low


def dot(a, b, a_dim=1):
    return lax.dot_general(a, b, (((a_dim,), (0,)), ((), ())), preferred_element_type=jnp.float32)


def butterflies(xs):
    xs = list(xs)
    step = 1
    while step < len(xs):
        for i in range(len(xs)):
            if not i & step:
                u, v = xs[i], xs[i | step]
                xs[i], xs[i | step] = (u, u) if v is None else (u + v, u - v)
        step *= 2
    return xs


def local_kernel(
    acts_ref, grads_ref, factor_ref, place_ref, lane_ref, sign_ref, out_ref, inner, whole, place, place_sem
):
    copy_in = pltpu.make_async_copy(place_ref, place, place_sem)
    copy_in.start()
    hidden, width = inner.shape
    blocks = hidden // TILE
    padded_blocks = GROUP_PAD // TILE
    strips = width // TILE
    matrix = sylvester(TILE)

    @pl.loop(0, blocks)
    def _(block):
        rows = pl.ds(pl.multiple_of(block * TILE, TILE), TILE)
        scaled = dot(acts_ref[:, rows], grads_ref[...], 0) * factor_ref[rows, :]
        parts = []
        for strip in range(strips):
            high, low = halves(scaled[:, strip * TILE : (strip + 1) * TILE])
            parts.append(dot(high, matrix) + dot(low, matrix))
        for strip, part in enumerate(butterflies(parts)):
            high, low = halves(part)
            inner[rows, strip * TILE : (strip + 1) * TILE] = dot(matrix, high) + dot(matrix, low)

    unrolled = 4

    @pl.loop(0, TILE // (unrolled * SUBLANES))
    def _(step):
        for strip in range(width // LANES):
            for piece in range(unrolled):
                start = pl.multiple_of((step * unrolled + piece) * SUBLANES, SUBLANES)
                xs = [None] * padded_blocks
                for block in range(blocks):
                    xs[block] = inner[
                        pl.ds(block * TILE + start, SUBLANES), strip * LANES : (strip + 1) * LANES
                    ]
                for block, x in enumerate(butterflies(xs)):
                    whole[pl.ds((strip * padded_blocks + block) * TILE + start, SUBLANES), :] = x

    copy_in.wait()
    lane_ids = lax.broadcasted_iota(jnp.int32, (SUBLANES, LANES), 1)
    sublane_ids = lax.broadcasted_iota(jnp.int32, (SUBLANES, LANES), 0)

    @pl.loop(0, out_ref.shape[0] // SUBLANES)
    def _(group):
        rows = pl.ds(pl.multiple_of(group * SUBLANES, SUBLANES), SUBLANES)
        lanes = lane_ref[rows, :]
        picked = jnp.zeros((SUBLANES, LANES), jnp.float32)
        for lane in range(LANES):
            held = None
            for sublane in range(SUBLANES):
                row = whole[pl.ds(place[(group * SUBLANES + sublane) * LANES + lane], 1), :]
                row = jnp.broadcast_to(row, (SUBLANES, LANES))
                held = row if held is None else jnp.where(sublane_ids == sublane, row, held)
            picked = jnp.where(lane_ids == lane, jnp.take_along_axis(held, lanes, axis=1), picked)
        out_ref[rows, :] = picked * sign_ref[rows, :]


def local_contributions(acts, grads, factor, place, lane, sign):
    hidden, width = factor.shape
    in_vmem = pl.BlockSpec(memory_space=pltpu.VMEM)
    return pl.pallas_call(
        local_kernel,
        out_shape=jax.ShapeDtypeStruct(sign.shape, jnp.float32),
        in_specs=[in_vmem] * 3 + [pl.BlockSpec(memory_space=pl.ANY)] + [in_vmem] * 2,
        out_specs=in_vmem,
        scratch_shapes=[
            pltpu.VMEM((hidden, width), jnp.float32),
            pltpu.VMEM((width // LANES * GROUP_PAD, LANES), jnp.float32),
            pltpu.SMEM(place.shape, jnp.int32),
            pltpu.SemaphoreType.DMA(()),
        ],
        compiler_params=pltpu.CompilerParams(vmem_limit_bytes=40 * 2**20),
    )(acts, grads, factor, place, lane, sign)


def gather_tokens(x, axis):
    copies = jnp.broadcast_to(x[None], (lax.axis_size(axis),) + x.shape)
    return lax.all_to_all(copies, axis, 0, 0, tiled=True).reshape(-1, x.shape[1])


def shards(hidden_acts, out_grads, second_moment, sign_flips, kept_rows, kept_cols):
    examples = hidden_acts.shape[0]
    devices = lax.axis_size("row") * lax.axis_size("col")
    my_row = lax.axis_index("row")
    my_col = lax.axis_index("col")
    hidden, width = second_moment.shape
    norm_scale = 1.0 / math.sqrt(ROWS_PAD * D)
    factor = sign_flips.astype(jnp.float32) / (jnp.sqrt(second_moment) + EPSILON) * norm_scale
    outs = []
    for example in range(examples):
        acts = gather_tokens(hidden_acts[example], "col")
        grads = gather_tokens(out_grads[example], "row")
        rows = kept_rows[example]
        cols = kept_cols[example]
        offset_col = cols % width
        place = offset_col // LANES * GROUP_PAD + rows % GROUP_PAD
        lane = (offset_col % LANES).reshape(devices, -1)
        flips = parity(rows // GROUP_PAD & my_row) ^ parity(cols // width & my_col)
        sign = (1 - 2 * flips).astype(jnp.float32).reshape(devices, -1)
        contribution = local_contributions(acts, grads, factor, place, lane, sign)
        received = lax.all_to_all(contribution, ("row", "col"), 0, 0, tiled=True)
        outs.append(jnp.sum(received, axis=0))
    return jnp.stack(outs)


def solution(mesh):
    placed = (
        P(None, "col", "row"),
        P(None, "row", "col"),
        P("row", "col"),
        P("row", "col"),
        P(),
        P(),
    )
    return jax.shard_map(
        shards, mesh=mesh, in_specs=placed, out_specs=P(None, ("row", "col")), check_vma=False
    )
```

time: 1330 us -> 106 us (0.08)
  waiting for transfers between devices: 865 us -> 30.8 us
  local copies, waits for them, and re-layouts: 255 us -> 7.45 us
  blocking collectives: 103 us -> 18 us
  matrix products: 77.7 us -> 0 us
  Pallas kernels: 0 us -> 24 us
  between operations: 13.7 us -> 0.05 us
    unnamed x4 -> x0, waiting for transfers between devices: 681 us -> none
    gather x1 -> x0, local copies, waits for them, and re-layouts: 192 us -> none  [shards(): picked = jnp.take_along_axis(shaped.reshape(examples, -1), position, axis=1)]
    all_gather x2 -> x0, waiting for transfers between devices: 90.6 us -> none  [the longest x1 49.3 us: shards(): grads_all = lax.all_gather(out_grads, 'row', axis=1, tiled=True)]
    all_to_all x1, blocking collectives: 103 us -> 18 us  [shards(): received = lax.all_to_all(contribution, ('row', 'col'), 0, 0, tiled=True)]
    dot_general x7 -> x0, matrix products: 77.7 us -> none  [the longest x1 15.9 us: rows_transform(): jnp.einsum('ij,eajm->eaim', sylvester(inner_len), shaped, precision=lax.P...]
    all_to_all x1 -> x2, waiting for transfers between devices: 92.5 us -> 30.8 us  [gather_tokens(): lax.all_to_all(copies, axis, 0, 0, tiled=True).reshape(-1, x.shape[1])]
    all_to_all x1 -> x0, local copies, waits for them, and re-layouts: 29.6 us -> none  [shards(): lax.all_to_all(transformed, 'row', split_axis=1, concat_axis=1, tiled=True)]
    pallas_call x0 -> x1, Pallas kernels: none -> 24 us  [local_contributions(): pl.pallas_call(local_kernel, out_shape=jax.ShapeDtypeStruct(sign.shape, j...]
  transfers between devices with their start and end apart: 4 -> 2, of which waited for: 4 -> 2; matrix products, arithmetic and copies ran while one was open for 0% -> 11% of each run, Pallas kernels for 0% -> 0%
where the time goes in v1:
time: 106 us; the launch traced here: 105 us
  waiting for transfers between devices  30.8 us (29%)
  Pallas kernels  24 us (23%)
  blocking collectives  18 us (17%)
  starting transfers between devices  12.7 us (12%)
  other arithmetic  11.7 us (11%)
  local copies, waits for them, and re-layouts  7.45 us (7%)
    all_to_all x2, waiting for transfers between devices, gather_tokens(): lax.all_to_all(copies, axis, 0, 0, tiled=True).reshape(-1, x.shape[1])  30.8 us
    pallas_call x1, Pallas kernels, local_contributions(): pl.pallas_call(local_kernel, out_shape=jax.ShapeDtypeStruct(sign.shape, j...  24 us
    all_to_all x1, blocking collectives, shards(): received = lax.all_to_all(contribution, ('row', 'col'), 0, 0, tiled=True)  18 us
    all_to_all x2, starting transfers between devices, gather_tokens(): lax.all_to_all(copies, axis, 0, 0, tiled=True).reshape(-1, x.shape[1])  12.7 us
    mul x1, other arithmetic, shards(): sign_flips.astype(jnp.float32) / (jnp.sqrt(second_moment) + EPSILON)  9.91 us
    broadcast_in_dim x2, local copies, waits for them, and re-layouts, gather_tokens(): copies = jnp.broadcast_to(x[None], (lax.axis_size(axis),) + x.shape)  4.36 us
    unnamed x6, local copies, waits for them, and re-layouts  3.09 us
  transfers between devices with their start and end apart: 2, of which 2 were waited for; matrix products, arithmetic and copies ran while one was open for 11% of the time, Pallas kernels for 0%

profile of v1, /device:TPU:0, one launch (start us, length us, event | category | flops | bytes accessed | tf_op | source)
XLA Modules:
  0.0 104.8 jit_solution(1534115468016410491)
XLA Ops:
  0.0 0.0 copy-start.1
  0.0 0.0 copy-start.2
  0.0 2.0 %broadcast_in_dim.17 = bf16[16,32,1024]{2,1,0:T(8,128)(2,1)} broadcast(bf16[32,1024]{1,0:T(8,128)(2,1)} %bitcast.20), dimensions={1,2} | broadcast | bytes 1114112 | tf_op jit(solution)/shard_map/broadcast_in_dim | solution.py:132
  2.0 7.8 %all-to-all-start.1 = ((bf16[16,32,1024]{2,1,0:T(8,128)(2,1)}), bf16[16,32,1024]{2,1,0:T(8,128)(2,1)S(1)}, u32[]{:S(2)}, u32[]{:S(2)}) async-start(bf16[16,32,1024]{2,1,0:T(8,128)(2,1)} %broadcast_in_dim.17), calls=%async_computation.1 | async-start | bytes 2097152 | tf_op jit(solution)/shard_map/all_to_all | solution.py:133
  9.8 1.1 %fusion.17 = (f32[128,128]{1,0:T(8,128)S(1)}, s32[128,128]{1,0:T(8,128)S(1)}) fusion(s32[128,128]{1,0:T(8,128)} %bitcast.17, s32[128,128]{1,0:T(8,128)} %bitcast.15, s32[]{:T(128)S(6)} %axis_index.25, s32[]{:T(128)S(6)} %axis_index.23), kind=kLoop, calls=%fused_computation.51 | loop fusion | flops 1130496 | bytes 262152 | tf_op jit(solution)/shard_map/convert_element_type | solution.py:154
  10.8 16.9 %all-to-all-done.1 = bf16[16,32,1024]{2,1,0:T(8,128)(2,1)S(1)} async-done(((bf16[16,32,1024]{2,1,0:T(8,128)(2,1)}), bf16[16,32,1024]{2,1,0:T(8,128)(2,1)S(1)}, u32[]{:S(2)}, u32[]{:S(2)}) %all-to-all-start.1) | async-done | bytes 1048608 | tf_op jit(solution)/shard_map/all_to_all | solution.py:133
  27.8 2.4 %broadcast_in_dim.15 = bf16[8,64,1792]{2,1,0:T(8,128)(2,1)} broadcast(bf16[64,1792]{1,0:T(8,128)(2,1)} %bitcast.19), dimensions={1,2} | broadcast | bytes 2064384 | tf_op jit(solution)/shard_map/broadcast_in_dim | solution.py:132
  30.2 4.9 %all-to-all-start = ((bf16[8,64,1792]{2,1,0:T(8,128)(2,1)}), bf16[8,64,1792]{2,1,0:T(8,128)(2,1)S(1)}, u32[]{:S(2)}, u32[]{:S(2)}) async-start(bf16[8,64,1792]{2,1,0:T(8,128)(2,1)} %broadcast_in_dim.15), calls=%async_computation | async-start | bytes 3670016 | tf_op jit(solution)/shard_map/all_to_all | solution.py:133
  35.1 0.0 copy-done.1
  35.1 0.0 copy-done.2
  35.1 0.1 fusion.3.place_ref
  35.2 9.9 %divide_multiply_fusion.factor_ref = f32[1792,1024]{1,0:T(8,128)} fusion(f32[1792,1024]{1,0:T(8,128)} %param.8, bf16[1792,1024]{1,0:T(8,128)(2,1)} %param.9), kind=kLoop, calls=%fused_computation | loop fusion | flops 7340032 | bytes 18350080 | tf_op jit(solution)/shard_map/mul | solution.py:143
  45.1 13.9 %all-to-all-done = bf16[8,64,1792]{2,1,0:T(8,128)(2,1)S(1)} async-done(((bf16[8,64,1792]{2,1,0:T(8,128)(2,1)}), bf16[8,64,1792]{2,1,0:T(8,128)(2,1)S(1)}, u32[]{:S(2)}, u32[]{:S(2)}) %all-to-all-start) | async-done | bytes 1835040 | tf_op jit(solution)/shard_map/all_to_all | solution.py:133
  59.0 0.0 copy-start
  59.0 3.1 %copy-done = f32[1792,1024]{1,0:T(8,128)S(1)} copy-done((f32[1792,1024]{1,0:T(8,128)S(1)}, f32[1792,1024]{1,0:T(8,128)}, u32[]{:S(2)}) %copy-start) | copy-done | bytes 7340056
  62.1 24.0 %shard_map.64 = f32[128,128]{1,0:T(8,128)S(1)} custom-call(bf16[512,1792]{1,0:T(8,128)(2,1)S(1)} %bitcast.12, bf16[512,1024]{1,0:T(8,128)(2,1)S(1)} %bitcast.13, f32[1792,1024]{1,0:T(8,128)S(1)} %copy-done, s32[16384]{0:T(1024)S(1)} %fusion.3.place_ref, s32[128,128]{1,0:T(8,128)S(1)} %get-tuple-element.6.lane_ref, f32[128,128]{1,0:T(8,128)S(1)} %get-tuple-element.5.sign_ref), custom_call_target="tpu_custom_call" | custom-call | tf_op jit(solution)/shard_map/pallas_call | solution.py:116
  86.1 18.0 %all_to_all.19 = f32[128,1,128]{2,1,0:T(1,128)S(1)} all-to-all(f32[128,1,128]{2,1,0:T(1,128)S(1)} %bitcast.14), channel_id=1, replica_groups=mesh['row'=16,'col'=8] {'row','col'}, dimensions={0} | all-to-all | bytes 131072 | tf_op jit(solution)/shard_map/all_to_all | solution.py:156
  104.1 0.7 reduce_sum.9
Async XLA Ops:
  0.0 35.1 %copy-start.1 = (s32[1,16384]{1,0:T(1,128)S(1)}, s32[1,16384]{1,0:T(1,128)}, u32[]{:S(2)}) copy-start(s32[1,16384]{1,0:T(1,128)} %param.10) | copy-start | bytes 196612
  0.0 35.1 %copy-start.2 = (s32[1,16384]{1,0:T(1,128)S(1)}, s32[1,16384]{1,0:T(1,128)}, u32[]{:S(2)}) copy-start(s32[1,16384]{1,0:T(1,128)} %param.11) | copy-start | bytes 196612
  2.0 25.8 %all-to-all-start.1 = ((bf16[16,32,1024]{2,1,0:T(8,128)(2,1)}), bf16[16,32,1024]{2,1,0:T(8,128)(2,1)S(1)}, u32[]{:S(2)}, u32[]{:S(2)}) async-start(bf16[16,32,1024]{2,1,0:T(8,128)(2,1)} %broadcast_in_dim.17), calls=%async_computation.1 | async-start | bytes 2097152 | tf_op jit(solution)/shard_map/all_to_all | solution.py:133
  30.2 28.9 %all-to-all-start = ((bf16[8,64,1792]{2,1,0:T(8,128)(2,1)}), bf16[8,64,1792]{2,1,0:T(8,128)(2,1)S(1)}, u32[]{:S(2)}, u32[]{:S(2)}) async-start(bf16[8,64,1792]{2,1,0:T(8,128)(2,1)} %broadcast_in_dim.15), calls=%async_computation | async-start | bytes 3670016 | tf_op jit(solution)/shard_map/all_to_all | solution.py:133
  59.0 3.1 %copy-start = (f32[1792,1024]{1,0:T(8,128)S(1)}, f32[1792,1024]{1,0:T(8,128)}, u32[]{:S(2)}) copy-start(f32[1792,1024]{1,0:T(8,128)} %divide_multiply_fusion.factor_ref) | copy-start | bytes 22020100

commit v2 on v1

--- a/solution.py
+++ b/solution.py
@@ -13,6 +13,7 @@
 GROUP_PAD = 2048
 ROWS_PAD = 32768
 EPSILON = 1e-08
+NORM_SCALE = 1.0 / math.sqrt(ROWS_PAD * D)
 
 LANES = 128
 SUBLANES = 8
@@ -53,13 +54,30 @@
     return xs
 
 
-def local_kernel(
-    acts_ref, grads_ref, factor_ref, place_ref, lane_ref, sign_ref, out_ref, inner, whole, place, place_sem
-):
+def local_kernel(masks, acts_ref, moment_ref, flips_ref, place_ref, lane_ref, sign_ref, *rest):
+    pieces, rest = rest[: len(masks)], rest[len(masks) :]
+    out_ref, grads_ref, moment, flips, inner, whole, place, place_sem, moment_sem, flips_sem = rest
+    blocks = inner.shape[0] // TILE
+    copies_in = []
+    for block in range(blocks):
+        rows = pl.ds(block * TILE, TILE)
+        for source, target, sem in (
+            (moment_ref, moment, moment_sem),
+            (flips_ref, flips, flips_sem),
+        ):
+            copies_in.append(
+                pltpu.make_async_copy(source.at[rows, :], target.at[rows, :], sem.at[block])
+            )
+            copies_in[-1].start()
     copy_in = pltpu.make_async_copy(place_ref, place, place_sem)
     copy_in.start()
-    hidden, width = inner.shape
-    blocks = hidden // TILE
+    mine = lax.axis_index("row")
+    for piece, piece_masks in zip(pieces, masks):
+        tokens = piece.shape[1]
+        for number, mask in enumerate(piece_masks):
+            start = pl.multiple_of((mine ^ mask) * tokens, tokens)
+            grads_ref[pl.ds(start, tokens), :] = piece[number]
+    width = inner.shape[1]
     padded_blocks = GROUP_PAD // TILE
     strips = width // TILE
     matrix = sylvester(TILE)
@@ -67,7 +85,13 @@
     @pl.loop(0, blocks)
     def _(block):
         rows = pl.ds(pl.multiple_of(block * TILE, TILE), TILE)
-        scaled = dot(acts_ref[:, rows], grads_ref[...], 0) * factor_ref[rows, :]
+        for source, target, sem in (
+            (moment_ref, moment, moment_sem),
+            (flips_ref, flips, flips_sem),
+        ):
+            pltpu.make_async_copy(source.at[rows, :], target.at[rows, :], sem.at[block]).wait()
+        factor = flips[rows, :].astype(jnp.float32) / (jnp.sqrt(moment[rows, :]) + EPSILON)
+        scaled = dot(acts_ref[:, rows], grads_ref[...], 0) * (factor * NORM_SCALE)
         parts = []
         for strip in range(strips):
             high, low = halves(scaled[:, strip * TILE : (strip + 1) * TILE])
@@ -110,27 +134,48 @@
         out_ref[rows, :] = picked * sign_ref[rows, :]
 
 
-def local_contributions(acts, grads, factor, place, lane, sign):
-    hidden, width = factor.shape
+def local_contributions(acts, grads, moment, flips, place, lane, sign):
+    hidden, width = moment.shape
+    masks, pieces = zip(*grads)
+    acts = acts.reshape(-1, hidden)
     in_vmem = pl.BlockSpec(memory_space=pltpu.VMEM)
+    anywhere = pl.BlockSpec(memory_space=pl.ANY)
     return pl.pallas_call(
-        local_kernel,
+        functools.partial(local_kernel, masks),
         out_shape=jax.ShapeDtypeStruct(sign.shape, jnp.float32),
-        in_specs=[in_vmem] * 3 + [pl.BlockSpec(memory_space=pl.ANY)] + [in_vmem] * 2,
+        in_specs=[in_vmem] + [anywhere] * 3 + [in_vmem] * (2 + len(pieces)),
         out_specs=in_vmem,
         scratch_shapes=[
+            pltpu.VMEM((acts.shape[0], width), jnp.bfloat16),
+            pltpu.VMEM((hidden, width), jnp.float32),
+            pltpu.VMEM((hidden, width), jnp.bfloat16),
             pltpu.VMEM((hidden, width), jnp.float32),
             pltpu.VMEM((width // LANES * GROUP_PAD, LANES), jnp.float32),
             pltpu.SMEM(place.shape, jnp.int32),
             pltpu.SemaphoreType.DMA(()),
+            pltpu.SemaphoreType.DMA((hidden // TILE,)),
+            pltpu.SemaphoreType.DMA((hidden // TILE,)),
         ],
-        compiler_params=pltpu.CompilerParams(vmem_limit_bytes=40 * 2**20),
-    )(acts, grads, factor, place, lane, sign)
-
-
-def gather_tokens(x, axis):
-    copies = jnp.broadcast_to(x[None], (lax.axis_size(axis),) + x.shape)
-    return lax.all_to_all(copies, axis, 0, 0, tiled=True).reshape(-1, x.shape[1])
+        compiler_params=pltpu.CompilerParams(vmem_limit_bytes=48 * 2**20),
+    )(acts, moment, flips, place, lane, sign, *pieces)
+
+
+def swap(x, axis, mask):
+    return lax.ppermute(x, axis, [(i, i ^ mask) for i in range(lax.axis_size(axis))])
+
+
+def gather_acts(x, after):
+    peers = lax.axis_size("col")
+    copies = jnp.broadcast_to(x[None], (peers,) + x.shape)
+    copies, after = lax.optimization_barrier((copies, after))
+    return lax.all_to_all(copies, "col", 0, 0, tiled=True)
+
+
+def gather_grads(pair):
+    half = jnp.concatenate([pair] + [swap(pair, "row", mask) for mask in (4, 12, 8)])
+    masks = tuple(far ^ near for far in (0, 4, 12, 8) for near in (0, 2))
+    other = swap(half, "row", 1)
+    return [(masks, half), (tuple(mask ^ 1 for mask in masks), other)]
 
 
 def shards(hidden_acts, out_grads, second_moment, sign_flips, kept_rows, kept_cols):
@@ -138,13 +183,13 @@
     devices = lax.axis_size("row") * lax.axis_size("col")
     my_row = lax.axis_index("row")
     my_col = lax.axis_index("col")
-    hidden, width = second_moment.shape
-    norm_scale = 1.0 / math.sqrt(ROWS_PAD * D)
-    factor = sign_flips.astype(jnp.float32) / (jnp.sqrt(second_moment) + EPSILON) * norm_scale
+    width = second_moment.shape[1]
     outs = []
     for example in range(examples):
-        acts = gather_tokens(hidden_acts[example], "col")
-        grads = gather_tokens(out_grads[example], "row")
+        own = out_grads[example][None]
+        pair = jnp.concatenate([own, swap(own, "row", 2)])
+        acts = gather_acts(hidden_acts[example], pair)
+        grads = gather_grads(pair)
         rows = kept_rows[example]
         cols = kept_cols[example]
         offset_col = cols % width
@@ -152,7 +197,9 @@
         lane = (offset_col % LANES).reshape(devices, -1)
         flips = parity(rows // GROUP_PAD & my_row) ^ parity(cols // width & my_col)
         sign = (1 - 2 * flips).astype(jnp.float32).reshape(devices, -1)
-        contribution = local_contributions(acts, grads, factor, place, lane, sign)
+        contribution = local_contributions(
+            acts, grads, second_moment, sign_flips, place, lane, sign
+        )
         received = lax.all_to_all(contribution, ("row", "col"), 0, 0, tiled=True)
         outs.append(jnp.sum(received, axis=0))
     return jnp.stack(outs)

time: 106 us -> 83.7 us (0.79)
  waiting for transfers between devices: 30.8 us -> 19.9 us
  other arithmetic: 11.7 us -> 0.94 us
  local copies, waits for them, and re-layouts: 7.45 us -> 3.25 us
  Pallas kernels: 24 us -> 27.2 us
    all_to_all x2 -> x1, waiting for transfers between devices: 30.8 us -> 10.9 us  [gather_acts(): return lax.all_to_all(copies, 'col', 0, 0, tiled=True)]
    mul x1 -> x0, other arithmetic: 9.91 us -> none  [shards(): sign_flips.astype(jnp.float32) / (jnp.sqrt(second_moment) + EPSILON)]
    ppermute x0 -> x5, waiting for transfers between devices: none -> 8.97 us  [swap(): lax.ppermute(x, axis, [(i, i ^ mask) for i in range(lax.axis_size(axis))])]
    ppermute x0 -> x5, starting transfers between devices: none -> 8.27 us  [swap(): lax.ppermute(x, axis, [(i, i ^ mask) for i in range(lax.axis_size(axis))])]
    all_to_all x2 -> x1, starting transfers between devices: 12.7 us -> 5.48 us  [gather_acts(): return lax.all_to_all(copies, 'col', 0, 0, tiled=True)]
    pallas_call x1, Pallas kernels: 24 us -> 27.2 us  [local_contributions(): pl.pallas_call(functools.partial(local_kernel, masks), out_shape=jax.Shap...]
    unnamed x6 -> x8, local copies, waits for them, and re-layouts: 3.09 us -> 0.92 us
    broadcast_in_dim x2 -> x1, local copies, waits for them, and re-layouts: 4.36 us -> 2.32 us  [gather_acts(): copies = jnp.broadcast_to(x[None], (peers,) + x.shape)]
  transfers between devices with their start and end apart: 2 -> 6, of which waited for: 2 -> 6; matrix products, arithmetic and copies ran while one was open for 11% -> 1% of each run, Pallas kernels for 0% -> 0%
where the time goes in v2:
time: 83.7 us; the launch traced here: 82.7 us
  Pallas kernels  27.2 us (32%)
  waiting for transfers between devices  19.9 us (24%)
  blocking collectives  17.6 us (21%)
  starting transfers between devices  13.7 us (16%)
  local copies, waits for them, and re-layouts  3.25 us (4%)
  other arithmetic  0.94 us (1%)
    pallas_call x1, Pallas kernels, local_contributions(): pl.pallas_call(functools.partial(local_kernel, masks), out_shape=jax.Shap...  27.2 us
    all_to_all x1, blocking collectives, shards(): received = lax.all_to_all(contribution, ('row', 'col'), 0, 0, tiled=True)  17.6 us
    all_to_all x1, waiting for transfers between devices, gather_acts(): return lax.all_to_all(copies, 'col', 0, 0, tiled=True)  10.9 us
    ppermute x5, waiting for transfers between devices, swap(): lax.ppermute(x, axis, [(i, i ^ mask) for i in range(lax.axis_size(axis))])  8.97 us
    ppermute x5, starting transfers between devices, swap(): lax.ppermute(x, axis, [(i, i ^ mask) for i in range(lax.axis_size(axis))])  8.27 us
    all_to_all x1, starting transfers between devices, gather_acts(): return lax.all_to_all(copies, 'col', 0, 0, tiled=True)  5.48 us
    broadcast_in_dim x1, local copies, waits for them, and re-layouts, gather_acts(): copies = jnp.broadcast_to(x[None], (peers,) + x.shape)  2.32 us
  transfers between devices with their start and end apart: 6, of which 6 were waited for; matrix products, arithmetic and copies ran while one was open for 1% of the time, Pallas kernels for 0%

profile of v2, /device:TPU:0, one launch (start us, length us, event | category | flops | bytes accessed | tf_op | source)
XLA Modules:
  0.0 82.7 jit_solution(14980574433470788578)
XLA Ops:
  0.0 0.0 copy-start.1
  0.0 0.0 copy-start
  0.0 4.0 %collective-permute-start = (bf16[1,32,1024]{2,1,0:T(8,128)(2,1)}, bf16[1,32,1024]{2,1,0:T(8,128)(2,1)S(1)}, u32[]{:S(2)}, u32[]{:S(2)}) collective-permute-start(bf16[1,32,1024]{2,1,0:T(8,128)(2,1)} %param.7), channel_id=1, source_target_pairs={{0,16},{8,24},{16,0},{24,8},{32,48},{40,56},{48,32},{56,40},{64,80... | collective-permute-start | bytes 196616 | tf_op jit(solution)/shard_map/ppermute | solution.py:164
  4.0 0.9 %constant_dynamic-update-slice_fusion.6 = (bf16[8,32,1024]{2,1,0:T(8,128)(2,1)S(1)}, bf16[2,32,1024]{2,1,0:T(8,128)(2,1)S(1)}) fusion(bf16[1,32,1024]{2,1,0:T(8,128)(2,1)} %param.7), kind=kLoop, calls=%fused_computation.58 | loop fusion | bytes 196608
  4.8 1.6 %collective-permute-done = bf16[1,32,1024]{2,1,0:T(8,128)(2,1)S(1)} collective-permute-done((bf16[1,32,1024]{2,1,0:T(8,128)(2,1)}, bf16[1,32,1024]{2,1,0:T(8,128)(2,1)S(1)}, u32[]{:S(2)}, u32[]{:S(2)}) %collective-permute-start) | collective-permute-done | bytes 65568 | tf_op jit(solution)/shard_map/ppermute | solution.py:164
  6.4 2.3 %broadcast_in_dim.8 = bf16[8,64,1792]{2,1,0:T(8,128)(2,1)} broadcast(bf16[64,1792]{1,0:T(8,128)(2,1)} %bitcast.16), dimensions={1,2} | broadcast | bytes 2064384 | tf_op jit(solution)/shard_map/broadcast_in_dim | solution.py:169
  8.8 5.5 %all-to-all-start = ((bf16[8,64,1792]{2,1,0:T(8,128)(2,1)}), bf16[8,64,1792]{2,1,0:T(8,128)(2,1)S(1)}, u32[]{:S(2)}, u32[]{:S(2)}) async-start(bf16[8,64,1792]{2,1,0:T(8,128)(2,1)} %broadcast_in_dim.8), calls=%async_computation | async-start | bytes 3670016 | tf_op jit(solution)/shard_map/all_to_all | solution.py:171
  14.2 1.5 %collective-permute-start.1 = (bf16[2,32,1024]{2,1,0:T(8,128)(2,1)S(1)}, bf16[2,32,1024]{2,1,0:T(8,128)(2,1)S(1)}, u32[]{:S(2)}, u32[]{:S(2)}) collective-permute-start(bf16[2,32,1024]{2,1,0:T(8,128)(2,1)S(1)} %get-tuple-element.8), channel_id=1, source_target_pairs={{0,32},{8,40},{16,48},{24,56},{32,0},{40,8},{48,16},{56,24},{64,96... | collective-permute-start | bytes 393224 | tf_op jit(solution)/shard_map/ppermute | solution.py:164
  15.7 2.1 %collective-permute-start.2 = (bf16[2,32,1024]{2,1,0:T(8,128)(2,1)S(1)}, bf16[2,32,1024]{2,1,0:T(8,128)(2,1)S(1)}, u32[]{:S(2)}, u32[]{:S(2)}) collective-permute-start(bf16[2,32,1024]{2,1,0:T(8,128)(2,1)S(1)} %get-tuple-element.8), channel_id=1, source_target_pairs={{0,96},{8,104},{16,112},{24,120},{32,64},{40,72},{48,80},{56,88},{... | collective-permute-start | bytes 393224 | tf_op jit(solution)/shard_map/ppermute | solution.py:164
  17.8 0.6 collective-permute-start.3
  18.5 1.8 %collective-permute-done.1 = bf16[2,32,1024]{2,1,0:T(8,128)(2,1)S(1)} collective-permute-done((bf16[2,32,1024]{2,1,0:T(8,128)(2,1)S(1)}, bf16[2,32,1024]{2,1,0:T(8,128)(2,1)S(1)}, u32[]{:S(2)}, u32[]{:S(2)}) %collective-permute-start.1) | collective-permute-done | bytes 131104 | tf_op jit(solution)/shard_map/ppermute | solution.py:164
  20.3 2.6 %collective-permute-done.2 = bf16[2,32,1024]{2,1,0:T(8,128)(2,1)S(1)} collective-permute-done((bf16[2,32,1024]{2,1,0:T(8,128)(2,1)S(1)}, bf16[2,32,1024]{2,1,0:T(8,128)(2,1)S(1)}, u32[]{:S(2)}, u32[]{:S(2)}) %collective-permute-start.2) | collective-permute-done | bytes 131104 | tf_op jit(solution)/shard_map/ppermute | solution.py:164
  22.8 1.5 %collective-permute-done.3 = bf16[2,32,1024]{2,1,0:T(8,128)(2,1)S(1)} collective-permute-done((bf16[2,32,1024]{2,1,0:T(8,128)(2,1)S(1)}, bf16[2,32,1024]{2,1,0:T(8,128)(2,1)S(1)}, u32[]{:S(2)}, u32[]{:S(2)}) %collective-permute-start.3) | collective-permute-done | bytes 131104 | tf_op jit(solution)/shard_map/ppermute | solution.py:164
  24.3 0.1 collective-permute-start.4
  24.4 0.0 copy-done.1
  24.4 0.0 copy-done
  24.4 0.2 fusion.17
  24.6 0.1 fusion.3.place_ref
  24.7 1.6 %collective-permute-done.4.rest_1_ = bf16[8,32,1024]{2,1,0:T(8,128)(2,1)S(1)} collective-permute-done((bf16[8,32,1024]{2,1,0:T(8,128)(2,1)S(1)}, bf16[8,32,1024]{2,1,0:T(8,128)(2,1)S(1)}, u32[]{:S(2)}, u32[]{:S(2)}) %collective-permute-start.4) | collective-permute-done | bytes 524320 | tf_op jit(solution)/shard_map/ppermute | solution.py:164
  26.3 10.9 %all-to-all-done = bf16[8,64,1792]{2,1,0:T(8,128)(2,1)S(1)} async-done(((bf16[8,64,1792]{2,1,0:T(8,128)(2,1)}), bf16[8,64,1792]{2,1,0:T(8,128)(2,1)S(1)}, u32[]{:S(2)}, u32[]{:S(2)}) %all-to-all-start) | async-done | bytes 1835040 | tf_op jit(solution)/shard_map/all_to_all | solution.py:171
  37.2 27.2 %shard_map.64 = f32[128,128]{1,0:T(8,128)S(1)} custom-call(bf16[512,1792]{1,0:T(8,128)(2,1)S(1)} %bitcast.10, f32[1792,1024]{1,0:T(8,128)} %moment_ref.1, bf16[1792,1024]{1,0:T(8,128)(2,1)} %flips_ref.1, s32[16384]{0:T(1024)S(1)} %fusion.3.place_ref, s32[128,128]{1,0:T(8,128)S(1)} %get-tuple-element.12.lane_ref, f32[128,128]{1,0:T(8,128)S(1)} %get-tuple-element.11.sign_ref, ...), custom_call_target="tpu_custom_call" | custom-call | tf_op jit(solution)/shard_map/pallas_call | solution.py:143
  64.5 17.6 %all_to_all.14 = f32[128,1,128]{2,1,0:T(1,128)S(1)} all-to-all(f32[128,1,128]{2,1,0:T(1,128)S(1)} %bitcast.11), channel_id=1, replica_groups=mesh['row'=16,'col'=8] {'row','col'}, dimensions={0} | all-to-all | bytes 131072 | tf_op jit(solution)/shard_map/all_to_all | solution.py:203
  82.1 0.7 reduce_sum.9
  (4 shorter events, 0.0 us)
Async XLA Ops:
  0.0 24.4 %copy-start.1 = (s32[1,16384]{1,0:T(1,128)S(1)}, s32[1,16384]{1,0:T(1,128)}, u32[]{:S(2)}) copy-start(s32[1,16384]{1,0:T(1,128)} %param.11) | copy-start | bytes 196612
  0.0 24.4 %copy-start = (s32[1,16384]{1,0:T(1,128)S(1)}, s32[1,16384]{1,0:T(1,128)}, u32[]{:S(2)}) copy-start(s32[1,16384]{1,0:T(1,128)} %param.10) | copy-start | bytes 196612
  0.0 6.4 %collective-permute-start = (bf16[1,32,1024]{2,1,0:T(8,128)(2,1)}, bf16[1,32,1024]{2,1,0:T(8,128)(2,1)S(1)}, u32[]{:S(2)}, u32[]{:S(2)}) collective-permute-start(bf16[1,32,1024]{2,1,0:T(8,128)(2,1)} %param.7), channel_id=1, source_target_pairs={{0,16},{8,24},{16,0},{24,8},{32,48},{40,56},{48,32},{56,40},{64,80... | collective-permute-start | bytes 196616 | tf_op jit(solution)/shard_map/ppermute | solution.py:164
  8.8 28.5 %all-to-all-start = ((bf16[8,64,1792]{2,1,0:T(8,128)(2,1)}), bf16[8,64,1792]{2,1,0:T(8,128)(2,1)S(1)}, u32[]{:S(2)}, u32[]{:S(2)}) async-start(bf16[8,64,1792]{2,1,0:T(8,128)(2,1)} %broadcast_in_dim.8), calls=%async_computation | async-start | bytes 3670016 | tf_op jit(solution)/shard_map/all_to_all | solution.py:171
  14.2 6.0 %collective-permute-start.1 = (bf16[2,32,1024]{2,1,0:T(8,128)(2,1)S(1)}, bf16[2,32,1024]{2,1,0:T(8,128)(2,1)S(1)}, u32[]{:S(2)}, u32[]{:S(2)}) collective-permute-start(bf16[2,32,1024]{2,1,0:T(8,128)(2,1)S(1)} %get-tuple-element.8), channel_id=1, source_target_pairs={{0,32},{8,40},{16,48},{24,56},{32,0},{40,8},{48,16},{56,24},{64,96... | collective-permute-start | bytes 393224 | tf_op jit(solution)/shard_map/ppermute | solution.py:164
  15.7 7.1 %collective-permute-start.2 = (bf16[2,32,1024]{2,1,0:T(8,128)(2,1)S(1)}, bf16[2,32,1024]{2,1,0:T(8,128)(2,1)S(1)}, u32[]{:S(2)}, u32[]{:S(2)}) collective-permute-start(bf16[2,32,1024]{2,1,0:T(8,128)(2,1)S(1)} %get-tuple-element.8), channel_id=1, source_target_pairs={{0,96},{8,104},{16,112},{24,120},{32,64},{40,72},{48,80},{56,88},{... | collective-permute-start | bytes 393224 | tf_op jit(solution)/shard_map/ppermute | solution.py:164
  17.8 6.5 %collective-permute-start.3 = (bf16[2,32,1024]{2,1,0:T(8,128)(2,1)S(1)}, bf16[2,32,1024]{2,1,0:T(8,128)(2,1)S(1)}, u32[]{:S(2)}, u32[]{:S(2)}) collective-permute-start(bf16[2,32,1024]{2,1,0:T(8,128)(2,1)S(1)} %get-tuple-element.8), channel_id=1, source_target_pairs={{0,64},{8,72},{16,80},{24,88},{32,96},{40,104},{48,112},{56,120},{... | collective-permute-start | bytes 393224 | tf_op jit(solution)/shard_map/ppermute | solution.py:164
  24.3 2.0 %collective-permute-start.4 = (bf16[8,32,1024]{2,1,0:T(8,128)(2,1)S(1)}, bf16[8,32,1024]{2,1,0:T(8,128)(2,1)S(1)}, u32[]{:S(2)}, u32[]{:S(2)}) collective-permute-start(bf16[8,32,1024]{2,1,0:T(8,128)(2,1)S(1)} %constant_dynamic-update-slice_fusion.2.rest_0_), channel_id=1, source_target_pairs={{0,8},{8,0},{16,24},{24,16},{32,40},{40,32},{48,56},{56,48},{64,72... | collective-permute-start | bytes 1572872 | tf_op jit(solution)/shard_map/ppermute | solution.py:164

commit v3 on v2

--- a/solution.py
+++ b/solution.py
@@ -18,6 +18,8 @@
 LANES = 128
 SUBLANES = 8
 TILE = 256
+CHUNK = 64
+PLACE_SLOTS = 4
 
 
 def parity(values):
@@ -56,49 +58,99 @@
 
 def local_kernel(masks, acts_ref, moment_ref, flips_ref, place_ref, lane_ref, sign_ref, *rest):
     pieces, rest = rest[: len(masks)], rest[len(masks) :]
-    out_ref, grads_ref, moment, flips, inner, whole, place, place_sem, moment_sem, flips_sem = rest
-    blocks = inner.shape[0] // TILE
-    copies_in = []
+    out_ref, grads_ref, moment, flips, scaled, half, inner, whole, *rest = rest
+    *places, moment_sem, flips_sem, place_sem = rest
+    hidden, width = inner.shape
+    blocks = hidden // TILE
+    padded_blocks = GROUP_PAD // TILE
+    strips = width // TILE
+    picks = SUBLANES * LANES
+    groups = out_ref.shape[0] // SUBLANES
+
+    def block_copies(block):
+        rows = pl.ds(pl.multiple_of(block * TILE, TILE), TILE)
+        return [
+            pltpu.make_async_copy(source.at[rows, :], target.at[rows, :], sem.at[block])
+            for source, target, sem in (
+                (moment_ref, moment, moment_sem),
+                (flips_ref, flips, flips_sem),
+            )
+        ]
+
+    def place_copy(group, slot):
+        return pltpu.make_async_copy(
+            place_ref.at[pl.ds(pl.multiple_of(group * picks, picks), picks)],
+            places[slot],
+            place_sem.at[slot],
+        )
+
     for block in range(blocks):
-        rows = pl.ds(block * TILE, TILE)
-        for source, target, sem in (
-            (moment_ref, moment, moment_sem),
-            (flips_ref, flips, flips_sem),
-        ):
-            copies_in.append(
-                pltpu.make_async_copy(source.at[rows, :], target.at[rows, :], sem.at[block])
-            )
-            copies_in[-1].start()
-    copy_in = pltpu.make_async_copy(place_ref, place, place_sem)
-    copy_in.start()
+        for copy in block_copies(block):
+            copy.start()
+    for slot in range(len(places)):
+        place_copy(slot, slot).start()
+
     mine = lax.axis_index("row")
     for piece, piece_masks in zip(pieces, masks):
         tokens = piece.shape[1]
         for number, mask in enumerate(piece_masks):
             start = pl.multiple_of((mine ^ mask) * tokens, tokens)
             grads_ref[pl.ds(start, tokens), :] = piece[number]
-    width = inner.shape[1]
-    padded_blocks = GROUP_PAD // TILE
-    strips = width // TILE
+
     matrix = sylvester(TILE)
-
-    @pl.loop(0, blocks)
+    matrix_beside = jnp.concatenate([matrix, matrix], axis=1)
+
+    def scale(block):
+        rows = pl.ds(pl.multiple_of(block * TILE, TILE), TILE)
+        acts = acts_ref[:, rows]
+        for strip in range(strips):
+            cols = slice(strip * TILE, (strip + 1) * TILE)
+            v = moment[rows, cols]
+            factor = flips[rows, cols].astype(jnp.float32) / (v * lax.rsqrt(v) + EPSILON)
+            scaled[:, cols] = dot(acts, grads_ref[:, cols], 0) * factor
+
+    def transform_cols():
+        for part in range(TILE // CHUNK):
+            part_rows = slice(part * CHUNK, (part + 1) * CHUNK)
+            xs = butterflies(
+                [scaled[part_rows, strip * TILE : (strip + 1) * TILE] for strip in range(strips)]
+            )
+            stacked = jnp.concatenate([y for x in xs for y in halves(x)], axis=0)
+            stacked = dot(stacked, matrix)
+            for strip in range(strips):
+                cols = slice(strip * TILE, (strip + 1) * TILE)
+                start = 2 * strip * CHUNK
+                x = stacked[start : start + CHUNK] + stacked[start + CHUNK : start + 2 * CHUNK]
+                high, low = halves(x)
+                half[part_rows, cols] = high
+                half[TILE + part * CHUNK : TILE + (part + 1) * CHUNK, cols] = low
+
+    def transform_rows(block):
+        rows = pl.ds(pl.multiple_of(block * TILE, TILE), TILE)
+        for strip in range(strips):
+            cols = slice(strip * TILE, (strip + 1) * TILE)
+            inner[rows, cols] = dot(matrix_beside, half[:, cols])
+
+    def wait_for(block):
+        for copy in block_copies(block):
+            copy.wait()
+
+    wait_for(0)
+    scale(0)
+    wait_for(1)
+    transform_cols()
+    scale(1)
+
+    @pl.loop(2, blocks)
     def _(block):
-        rows = pl.ds(pl.multiple_of(block * TILE, TILE), TILE)
-        for source, target, sem in (
-            (moment_ref, moment, moment_sem),
-            (flips_ref, flips, flips_sem),
-        ):
-            pltpu.make_async_copy(source.at[rows, :], target.at[rows, :], sem.at[block]).wait()
-        factor = flips[rows, :].astype(jnp.float32) / (jnp.sqrt(moment[rows, :]) + EPSILON)
-        scaled = dot(acts_ref[:, rows], grads_ref[...], 0) * (factor * NORM_SCALE)
-        parts = []
-        for strip in range(strips):
-            high, low = halves(scaled[:, strip * TILE : (strip + 1) * TILE])
-            parts.append(dot(high, matrix) + dot(low, matrix))
-        for strip, part in enumerate(butterflies(parts)):
-            high, low = halves(part)
-            inner[rows, strip * TILE : (strip + 1) * TILE] = dot(matrix, high) + dot(matrix, low)
+        wait_for(block)
+        transform_rows(block - 2)
+        transform_cols()
+        scale(block)
+
+    transform_rows(blocks - 2)
+    transform_cols()
+    transform_rows(blocks - 1)
 
     unrolled = 4
 
@@ -115,23 +167,29 @@
                 for block, x in enumerate(butterflies(xs)):
                     whole[pl.ds((strip * padded_blocks + block) * TILE + start, SUBLANES), :] = x
 
-    copy_in.wait()
     lane_ids = lax.broadcasted_iota(jnp.int32, (SUBLANES, LANES), 1)
     sublane_ids = lax.broadcasted_iota(jnp.int32, (SUBLANES, LANES), 0)
 
-    @pl.loop(0, out_ref.shape[0] // SUBLANES)
-    def _(group):
-        rows = pl.ds(pl.multiple_of(group * SUBLANES, SUBLANES), SUBLANES)
-        lanes = lane_ref[rows, :]
-        picked = jnp.zeros((SUBLANES, LANES), jnp.float32)
-        for lane in range(LANES):
-            held = None
-            for sublane in range(SUBLANES):
-                row = whole[pl.ds(place[(group * SUBLANES + sublane) * LANES + lane], 1), :]
-                row = jnp.broadcast_to(row, (SUBLANES, LANES))
-                held = row if held is None else jnp.where(sublane_ids == sublane, row, held)
-            picked = jnp.where(lane_ids == lane, jnp.take_along_axis(held, lanes, axis=1), picked)
-        out_ref[rows, :] = picked * sign_ref[rows, :]
+    @pl.loop(0, groups // len(places))
+    def _(step):
+        for slot, place in enumerate(places):
+            group = step * len(places) + slot
+            place_copy(group, slot).wait()
+            rows = pl.ds(pl.multiple_of(group * SUBLANES, SUBLANES), SUBLANES)
+            lanes = lane_ref[rows, :]
+            picked = jnp.zeros((SUBLANES, LANES), jnp.float32)
+            for lane in range(LANES):
+                held = None
+                for sublane in range(SUBLANES):
+                    row = whole[pl.ds(place[sublane * LANES + lane], 1), :]
+                    row = jnp.broadcast_to(row, (SUBLANES, LANES))
+                    held = row if held is None else jnp.where(sublane_ids == sublane, row, held)
+                picked = jnp.where(lane_ids == lane, jnp.take_along_axis(held, lanes, axis=1), picked)
+            out_ref[rows, :] = picked * sign_ref[rows, :]
+
+            @pl.when(group + len(places) < groups)
+            def _():
+                place_copy(group + len(places), slot).start()
 
 
 def local_contributions(acts, grads, moment, flips, place, lane, sign):
@@ -149,12 +207,14 @@
             pltpu.VMEM((acts.shape[0], width), jnp.bfloat16),
             pltpu.VMEM((hidden, width), jnp.float32),
             pltpu.VMEM((hidden, width), jnp.bfloat16),
+            pltpu.VMEM((TILE, width), jnp.float32),
+            pltpu.VMEM((2 * TILE, width), jnp.bfloat16),
             pltpu.VMEM((hidden, width), jnp.float32),
             pltpu.VMEM((width // LANES * GROUP_PAD, LANES), jnp.float32),
-            pltpu.SMEM(place.shape, jnp.int32),
-            pltpu.SemaphoreType.DMA(()),
+            *[pltpu.SMEM((SUBLANES * LANES,), jnp.int32)] * PLACE_SLOTS,
             pltpu.SemaphoreType.DMA((hidden // TILE,)),
             pltpu.SemaphoreType.DMA((hidden // TILE,)),
+            pltpu.SemaphoreType.DMA((PLACE_SLOTS,)),
         ],
         compiler_params=pltpu.CompilerParams(vmem_limit_bytes=48 * 2**20),
     )(acts, moment, flips, place, lane, sign, *pieces)
@@ -196,7 +256,7 @@
         place = offset_col // LANES * GROUP_PAD + rows % GROUP_PAD
         lane = (offset_col % LANES).reshape(devices, -1)
         flips = parity(rows // GROUP_PAD & my_row) ^ parity(cols // width & my_col)
-        sign = (1 - 2 * flips).astype(jnp.float32).reshape(devices, -1)
+        sign = ((1 - 2 * flips).astype(jnp.float32) * NORM_SCALE).reshape(devices, -1)
         contribution = local_contributions(
             acts, grads, second_moment, sign_flips, place, lane, sign
         )

time: 83.7 us -> 77.1 us (0.921)
  Pallas kernels: 27.2 us -> 20.7 us
    pallas_call x1, Pallas kernels: 27.2 us -> 20.7 us  [local_contributions(): pl.pallas_call(functools.partial(local_kernel, masks), out_shape=jax.Shap...]
  transfers between devices with their start and end apart: 6 -> 6, of which waited for: 6 -> 6; matrix products, arithmetic and copies ran while one was open for 1% -> 2% of each run, Pallas kernels for 0% -> 0%
where the time goes in v3:
time: 77.1 us; the launch traced here: 76.2 us
  Pallas kernels  20.7 us (27%)
  waiting for transfers between devices  19.8 us (26%)
  blocking collectives  17.6 us (23%)
  starting transfers between devices  13.8 us (18%)
  local copies, waits for them, and re-layouts  3.23 us (4%)
  other arithmetic  0.95 us (1%)
    pallas_call x1, Pallas kernels, local_contributions(): pl.pallas_call(functools.partial(local_kernel, masks), out_shape=jax.Shap...  20.7 us
    all_to_all x1, blocking collectives, shards(): received = lax.all_to_all(contribution, ('row', 'col'), 0, 0, tiled=True)  17.6 us
    all_to_all x1, waiting for transfers between devices, gather_acts(): return lax.all_to_all(copies, 'col', 0, 0, tiled=True)  10.7 us
    ppermute x5, waiting for transfers between devices, swap(): lax.ppermute(x, axis, [(i, i ^ mask) for i in range(lax.axis_size(axis))])  9.1 us
    ppermute x5, starting transfers between devices, swap(): lax.ppermute(x, axis, [(i, i ^ mask) for i in range(lax.axis_size(axis))])  8.36 us
    all_to_all x1, starting transfers between devices, gather_acts(): return lax.all_to_all(copies, 'col', 0, 0, tiled=True)  5.48 us
    broadcast_in_dim x1, local copies, waits for them, and re-layouts, gather_acts(): copies = jnp.broadcast_to(x[None], (peers,) + x.shape)  2.31 us
  transfers between devices with their start and end apart: 6, of which 6 were waited for; matrix products, arithmetic and copies ran while one was open for 2% of the time, Pallas kernels for 0%

profile of v3, /device:TPU:0, one launch (start us, length us, event | category | flops | bytes accessed | tf_op | source)
XLA Modules:
  0.0 76.2 jit_solution(12419890559508454908)
XLA Ops:
  0.0 0.0 copy-start
  0.0 0.0 copy-start.1
  0.0 4.0 %collective-permute-start = (bf16[1,32,1024]{2,1,0:T(8,128)(2,1)}, bf16[1,32,1024]{2,1,0:T(8,128)(2,1)S(1)}, u32[]{:S(2)}, u32[]{:S(2)}) collective-permute-start(bf16[1,32,1024]{2,1,0:T(8,128)(2,1)} %param.7), channel_id=1, source_target_pairs={{0,16},{8,24},{16,0},{24,8},{32,48},{40,56},{48,32},{56,40},{64,80... | collective-permute-start | bytes 196616 | tf_op jit(solution)/shard_map/ppermute | solution.py:224
  4.0 0.9 %constant_dynamic-update-slice_fusion.6 = (bf16[8,32,1024]{2,1,0:T(8,128)(2,1)S(1)}, bf16[2,32,1024]{2,1,0:T(8,128)(2,1)S(1)}) fusion(bf16[1,32,1024]{2,1,0:T(8,128)(2,1)} %param.7), kind=kLoop, calls=%fused_computation.58 | loop fusion | bytes 196608
  4.8 1.6 %collective-permute-done = bf16[1,32,1024]{2,1,0:T(8,128)(2,1)S(1)} collective-permute-done((bf16[1,32,1024]{2,1,0:T(8,128)(2,1)}, bf16[1,32,1024]{2,1,0:T(8,128)(2,1)S(1)}, u32[]{:S(2)}, u32[]{:S(2)}) %collective-permute-start) | collective-permute-done | bytes 65568 | tf_op jit(solution)/shard_map/ppermute | solution.py:224
  6.4 2.3 %broadcast_in_dim.8 = bf16[8,64,1792]{2,1,0:T(8,128)(2,1)} broadcast(bf16[64,1792]{1,0:T(8,128)(2,1)} %bitcast.17), dimensions={1,2} | broadcast | bytes 2064384 | tf_op jit(solution)/shard_map/broadcast_in_dim | solution.py:229
  8.7 5.5 %all-to-all-start = ((bf16[8,64,1792]{2,1,0:T(8,128)(2,1)}), bf16[8,64,1792]{2,1,0:T(8,128)(2,1)S(1)}, u32[]{:S(2)}, u32[]{:S(2)}) async-start(bf16[8,64,1792]{2,1,0:T(8,128)(2,1)} %broadcast_in_dim.8), calls=%async_computation | async-start | bytes 3670016 | tf_op jit(solution)/shard_map/all_to_all | solution.py:231
  14.2 1.5 %collective-permute-start.1 = (bf16[2,32,1024]{2,1,0:T(8,128)(2,1)S(1)}, bf16[2,32,1024]{2,1,0:T(8,128)(2,1)S(1)}, u32[]{:S(2)}, u32[]{:S(2)}) collective-permute-start(bf16[2,32,1024]{2,1,0:T(8,128)(2,1)S(1)} %get-tuple-element.8), channel_id=1, source_target_pairs={{0,32},{8,40},{16,48},{24,56},{32,0},{40,8},{48,16},{56,24},{64,96... | collective-permute-start | bytes 393224 | tf_op jit(solution)/shard_map/ppermute | solution.py:224
  15.7 2.1 %collective-permute-start.2 = (bf16[2,32,1024]{2,1,0:T(8,128)(2,1)S(1)}, bf16[2,32,1024]{2,1,0:T(8,128)(2,1)S(1)}, u32[]{:S(2)}, u32[]{:S(2)}) collective-permute-start(bf16[2,32,1024]{2,1,0:T(8,128)(2,1)S(1)} %get-tuple-element.8), channel_id=1, source_target_pairs={{0,96},{8,104},{16,112},{24,120},{32,64},{40,72},{48,80},{56,88},{... | collective-permute-start | bytes 393224 | tf_op jit(solution)/shard_map/ppermute | solution.py:224
  17.8 0.0 copy-done
  17.8 0.0 copy-done.1
  17.8 0.1 convert_multiply_fusion.sign_ref
  17.9 0.7 collective-permute-start.3
  18.7 1.3 %collective-permute-done.1 = bf16[2,32,1024]{2,1,0:T(8,128)(2,1)S(1)} collective-permute-done((bf16[2,32,1024]{2,1,0:T(8,128)(2,1)S(1)}, bf16[2,32,1024]{2,1,0:T(8,128)(2,1)S(1)}, u32[]{:S(2)}, u32[]{:S(2)}) %collective-permute-start.1) | collective-permute-done | bytes 131104 | tf_op jit(solution)/shard_map/ppermute | solution.py:224
  20.0 3.0 %collective-permute-done.2 = bf16[2,32,1024]{2,1,0:T(8,128)(2,1)S(1)} collective-permute-done((bf16[2,32,1024]{2,1,0:T(8,128)(2,1)S(1)}, bf16[2,32,1024]{2,1,0:T(8,128)(2,1)S(1)}, u32[]{:S(2)}, u32[]{:S(2)}) %collective-permute-start.2) | collective-permute-done | bytes 131104 | tf_op jit(solution)/shard_map/ppermute | solution.py:224
  23.0 1.5 %collective-permute-done.3 = bf16[2,32,1024]{2,1,0:T(8,128)(2,1)S(1)} collective-permute-done((bf16[2,32,1024]{2,1,0:T(8,128)(2,1)S(1)}, bf16[2,32,1024]{2,1,0:T(8,128)(2,1)S(1)}, u32[]{:S(2)}, u32[]{:S(2)}) %collective-permute-start.3) | collective-permute-done | bytes 131104 | tf_op jit(solution)/shard_map/ppermute | solution.py:224
  24.5 0.1 collective-permute-start.4
  24.6 0.1 add_select_fusion.2.lane_ref
  24.7 0.1 fusion.3.place_ref
  24.8 1.7 %collective-permute-done.4.rest_1_ = bf16[8,32,1024]{2,1,0:T(8,128)(2,1)S(1)} collective-permute-done((bf16[8,32,1024]{2,1,0:T(8,128)(2,1)S(1)}, bf16[8,32,1024]{2,1,0:T(8,128)(2,1)S(1)}, u32[]{:S(2)}, u32[]{:S(2)}) %collective-permute-start.4) | collective-permute-done | bytes 524320 | tf_op jit(solution)/shard_map/ppermute | solution.py:224
  26.5 10.7 %all-to-all-done = bf16[8,64,1792]{2,1,0:T(8,128)(2,1)S(1)} async-done(((bf16[8,64,1792]{2,1,0:T(8,128)(2,1)}), bf16[8,64,1792]{2,1,0:T(8,128)(2,1)S(1)}, u32[]{:S(2)}, u32[]{:S(2)}) %all-to-all-start) | async-done | bytes 1835040 | tf_op jit(solution)/shard_map/all_to_all | solution.py:231
  37.2 20.7 %shard_map.64 = f32[128,128]{1,0:T(8,128)S(1)} custom-call(bf16[512,1792]{1,0:T(8,128)(2,1)S(1)} %bitcast.10, f32[1792,1024]{1,0:T(8,128)} %moment_ref.1, bf16[1792,1024]{1,0:T(8,128)(2,1)} %flips_ref.1, s32[16384]{0:T(1024)S(1)} %fusion.3.place_ref, s32[128,128]{1,0:T(8,128)S(1)} %add_select_fusion.2.lane_ref, ...), custom_call_target="tpu_custom_call" | custom-call | tf_op jit(solution)/shard_map/pallas_call | solution.py:201
  57.9 17.6 %all_to_all.14 = f32[128,1,128]{2,1,0:T(1,128)S(1)} all-to-all(f32[128,1,128]{2,1,0:T(1,128)S(1)} %bitcast.11), channel_id=1, replica_groups=mesh['row'=16,'col'=8] {'row','col'}, dimensions={0} | all-to-all | bytes 131072 | tf_op jit(solution)/shard_map/all_to_all | solution.py:263
  75.5 0.7 reduce_sum.9
  (4 shorter events, 0.0 us)
Async XLA Ops:
  0.0 17.8 %copy-start = (s32[1,16384]{1,0:T(1,128)S(1)}, s32[1,16384]{1,0:T(1,128)}, u32[]{:S(2)}) copy-start(s32[1,16384]{1,0:T(1,128)} %param.11) | copy-start | bytes 196612
  0.0 17.8 %copy-start.1 = (s32[1,16384]{1,0:T(1,128)S(1)}, s32[1,16384]{1,0:T(1,128)}, u32[]{:S(2)}) copy-start(s32[1,16384]{1,0:T(1,128)} %param.10) | copy-start | bytes 196612
  0.0 6.4 %collective-permute-start = (bf16[1,32,1024]{2,1,0:T(8,128)(2,1)}, bf16[1,32,1024]{2,1,0:T(8,128)(2,1)S(1)}, u32[]{:S(2)}, u32[]{:S(2)}) collective-permute-start(bf16[1,32,1024]{2,1,0:T(8,128)(2,1)} %param.7), channel_id=1, source_target_pairs={{0,16},{8,24},{16,0},{24,8},{32,48},{40,56},{48,32},{56,40},{64,80... | collective-permute-start | bytes 196616 | tf_op jit(solution)/shard_map/ppermute | solution.py:224
  8.7 28.5 %all-to-all-start = ((bf16[8,64,1792]{2,1,0:T(8,128)(2,1)}), bf16[8,64,1792]{2,1,0:T(8,128)(2,1)S(1)}, u32[]{:S(2)}, u32[]{:S(2)}) async-start(bf16[8,64,1792]{2,1,0:T(8,128)(2,1)} %broadcast_in_dim.8), calls=%async_computation | async-start | bytes 3670016 | tf_op jit(solution)/shard_map/all_to_all | solution.py:231
  14.2 5.8 %collective-permute-start.1 = (bf16[2,32,1024]{2,1,0:T(8,128)(2,1)S(1)}, bf16[2,32,1024]{2,1,0:T(8,128)(2,1)S(1)}, u32[]{:S(2)}, u32[]{:S(2)}) collective-permute-start(bf16[2,32,1024]{2,1,0:T(8,128)(2,1)S(1)} %get-tuple-element.8), channel_id=1, source_target_pairs={{0,32},{8,40},{16,48},{24,56},{32,0},{40,8},{48,16},{56,24},{64,96... | collective-permute-start | bytes 393224 | tf_op jit(solution)/shard_map/ppermute | solution.py:224
  15.7 7.3 %collective-permute-start.2 = (bf16[2,32,1024]{2,1,0:T(8,128)(2,1)S(1)}, bf16[2,32,1024]{2,1,0:T(8,128)(2,1)S(1)}, u32[]{:S(2)}, u32[]{:S(2)}) collective-permute-start(bf16[2,32,1024]{2,1,0:T(8,128)(2,1)S(1)} %get-tuple-element.8), channel_id=1, source_target_pairs={{0,96},{8,104},{16,112},{24,120},{32,64},{40,72},{48,80},{56,88},{... | collective-permute-start | bytes 393224 | tf_op jit(solution)/shard_map/ppermute | solution.py:224
  17.9 6.6 %collective-permute-start.3 = (bf16[2,32,1024]{2,1,0:T(8,128)(2,1)S(1)}, bf16[2,32,1024]{2,1,0:T(8,128)(2,1)S(1)}, u32[]{:S(2)}, u32[]{:S(2)}) collective-permute-start(bf16[2,32,1024]{2,1,0:T(8,128)(2,1)S(1)} %get-tuple-element.8), channel_id=1, source_target_pairs={{0,64},{8,72},{16,80},{24,88},{32,96},{40,104},{48,112},{56,120},{... | collective-permute-start | bytes 393224 | tf_op jit(solution)/shard_map/ppermute | solution.py:224
  24.5 2.0 %collective-permute-start.4 = (bf16[8,32,1024]{2,1,0:T(8,128)(2,1)S(1)}, bf16[8,32,1024]{2,1,0:T(8,128)(2,1)S(1)}, u32[]{:S(2)}, u32[]{:S(2)}) collective-permute-start(bf16[8,32,1024]{2,1,0:T(8,128)(2,1)S(1)} %constant_dynamic-update-slice_fusion.2.rest_0_), channel_id=1, source_target_pairs={{0,8},{8,0},{16,24},{24,16},{32,40},{40,32},{48,56},{56,48},{64,72... | collective-permute-start | bytes 1572872 | tf_op jit(solution)/shard_map/ppermute | solution.py:224

commit v4 on v3

--- a/solution.py
+++ b/solution.py
@@ -56,15 +56,18 @@
     return xs
 
 
-def local_kernel(masks, acts_ref, moment_ref, flips_ref, place_ref, lane_ref, sign_ref, *rest):
-    pieces, rest = rest[: len(masks)], rest[len(masks) :]
-    out_ref, grads_ref, moment, flips, scaled, half, inner, whole, *rest = rest
+def local_kernel(
+    example, acts_masks, grads_masks, own_acts, moment_ref, flips_ref, place_ref, lane_ref, sign_ref, *rest
+):
+    acts_pieces, rest = rest[: len(acts_masks)], rest[len(acts_masks) :]
+    grads_pieces, rest = rest[: len(grads_masks)], rest[len(grads_masks) :]
+    out_ref, acts_ref, grads_ref, moment, flips, scaled, half, inner, whole, *rest = rest
+    own_sem, *rest = rest
     *places, moment_sem, flips_sem, place_sem = rest
     hidden, width = inner.shape
     blocks = hidden // TILE
     padded_blocks = GROUP_PAD // TILE
     strips = width // TILE
-    picks = SUBLANES * LANES
     groups = out_ref.shape[0] // SUBLANES
 
     def block_copies(block):
@@ -79,23 +82,34 @@
 
     def place_copy(group, slot):
         return pltpu.make_async_copy(
-            place_ref.at[pl.ds(pl.multiple_of(group * picks, picks), picks)],
+            place_ref.at[pl.ds(pl.multiple_of(group * SUBLANES, SUBLANES), SUBLANES), :],
             places[slot],
             place_sem.at[slot],
         )
 
+
+    own_tokens = own_acts.shape[1]
+    own_start = pl.multiple_of(lax.axis_index("col") * own_tokens, own_tokens)
+    own_copy = pltpu.make_async_copy(
+        own_acts.at[example], acts_ref.at[pl.ds(own_start, own_tokens), :], own_sem
+    )
+    own_copy.start()
     for block in range(blocks):
         for copy in block_copies(block):
             copy.start()
     for slot in range(len(places)):
         place_copy(slot, slot).start()
-
-    mine = lax.axis_index("row")
-    for piece, piece_masks in zip(pieces, masks):
-        tokens = piece.shape[1]
-        for number, mask in enumerate(piece_masks):
-            start = pl.multiple_of((mine ^ mask) * tokens, tokens)
-            grads_ref[pl.ds(start, tokens), :] = piece[number]
+    for axis, target, masks, pieces in (
+        ("col", acts_ref, acts_masks, acts_pieces),
+        ("row", grads_ref, grads_masks, grads_pieces),
+    ):
+        mine = lax.axis_index(axis)
+        for piece, piece_masks in zip(pieces, masks):
+            tokens = piece.shape[1]
+            for number, mask in enumerate(piece_masks):
+                start = pl.multiple_of((mine ^ mask) * tokens, tokens)
+                target[pl.ds(start, tokens), :] = piece[number]
+    own_copy.wait()
 
     matrix = sylvester(TILE)
     matrix_beside = jnp.concatenate([matrix, matrix], axis=1)
@@ -181,7 +195,7 @@
             for lane in range(LANES):
                 held = None
                 for sublane in range(SUBLANES):
-                    row = whole[pl.ds(place[sublane * LANES + lane], 1), :]
+                    row = whole[pl.ds(place[sublane, lane], 1), :]
                     row = jnp.broadcast_to(row, (SUBLANES, LANES))
                     held = row if held is None else jnp.where(sublane_ids == sublane, row, held)
                 picked = jnp.where(lane_ids == lane, jnp.take_along_axis(held, lanes, axis=1), picked)
@@ -192,50 +206,60 @@
                 place_copy(group + len(places), slot).start()
 
 
-def local_contributions(acts, grads, moment, flips, place, lane, sign):
+def local_contributions(example, hidden_acts, acts, grads, moment, flips, place, lane, sign):
     hidden, width = moment.shape
-    masks, pieces = zip(*grads)
-    acts = acts.reshape(-1, hidden)
+    acts_masks, acts = zip(*acts)
+    grads_masks, grads = zip(*grads)
+    tokens = hidden_acts.shape[1] + sum(x.shape[0] * x.shape[1] for x in acts)
     in_vmem = pl.BlockSpec(memory_space=pltpu.VMEM)
-    anywhere = pl.BlockSpec(memory_space=pl.ANY)
+    in_hbm = pl.BlockSpec(memory_space=pltpu.HBM)
     return pl.pallas_call(
-        functools.partial(local_kernel, masks),
-        out_shape=jax.ShapeDtypeStruct(sign.shape, jnp.float32),
-        in_specs=[in_vmem] + [anywhere] * 3 + [in_vmem] * (2 + len(pieces)),
+        functools.partial(local_kernel, example, acts_masks, grads_masks),
+        out_shape=jax.ShapeDtypeStruct(place.shape, jnp.float32),
+        in_specs=[in_hbm] * 3 + [in_vmem] * (3 +  len(acts) + len(grads)),
         out_specs=in_vmem,
         scratch_shapes=[
-            pltpu.VMEM((acts.shape[0], width), jnp.bfloat16),
+            pltpu.VMEM((tokens, hidden), jnp.bfloat16),
+            pltpu.VMEM((tokens, width), jnp.bfloat16),
             pltpu.VMEM((hidden, width), jnp.float32),
             pltpu.VMEM((hidden, width), jnp.bfloat16),
             pltpu.VMEM((TILE, width), jnp.float32),
             pltpu.VMEM((2 * TILE, width), jnp.bfloat16),
             pltpu.VMEM((hidden, width), jnp.float32),
             pltpu.VMEM((width // LANES * GROUP_PAD, LANES), jnp.float32),
-            *[pltpu.SMEM((SUBLANES * LANES,), jnp.int32)] * PLACE_SLOTS,
+            pltpu.SemaphoreType.DMA(()),
+            *[pltpu.SMEM((SUBLANES, LANES), jnp.int32)] * PLACE_SLOTS,
             pltpu.SemaphoreType.DMA((hidden // TILE,)),
             pltpu.SemaphoreType.DMA((hidden // TILE,)),
             pltpu.SemaphoreType.DMA((PLACE_SLOTS,)),
         ],
         compiler_params=pltpu.CompilerParams(vmem_limit_bytes=48 * 2**20),
-    )(acts, moment, flips, place, lane, sign, *pieces)
+    )(hidden_acts, moment, flips, place, lane, sign, *acts, *grads)
 
 
 def swap(x, axis, mask):
     return lax.ppermute(x, axis, [(i, i ^ mask) for i in range(lax.axis_size(axis))])
 
 
-def gather_acts(x, after):
-    peers = lax.axis_size("col")
-    copies = jnp.broadcast_to(x[None], (peers,) + x.shape)
-    copies, after = lax.optimization_barrier((copies, after))
-    return lax.all_to_all(copies, "col", 0, 0, tiled=True)
-
-
-def gather_grads(pair):
+def gather(acts, grads, meanwhile):
+    own = grads[None]
+    near = swap(own, "row", 2)
+    held = {0: acts[None]}
+    for mask in (4, 1, 3):
+        held[mask] = swap(held[0], "col", mask)
+    far = swap(held[0], "col", 6)
+    held, near, meanwhile = lax.optimization_barrier((held, near, meanwhile))
+    held[5] = swap(held[4], "col", 1)
+    held[2] = swap(held[1], "col", 3)
+    held[7] = swap(held[3], "col", 4)
+    held[6] = far
+    pair = jnp.concatenate([own, near])
     half = jnp.concatenate([pair] + [swap(pair, "row", mask) for mask in (4, 12, 8)])
+    held, half = lax.optimization_barrier((held, half))
+    other = swap(half, "row", 1)
+    acts = [((mask,), piece) for mask, piece in held.items() if mask]
     masks = tuple(far ^ near for far in (0, 4, 12, 8) for near in (0, 2))
-    other = swap(half, "row", 1)
-    return [(masks, half), (tuple(mask ^ 1 for mask in masks), other)]
+    return acts, [(masks, half), (tuple(mask ^ 1 for mask in masks), other)], meanwhile
 
 
 def shards(hidden_acts, out_grads, second_moment, sign_flips, kept_rows, kept_cols):
@@ -246,19 +270,15 @@
     width = second_moment.shape[1]
     outs = []
     for example in range(examples):
-        own = out_grads[example][None]
-        pair = jnp.concatenate([own, swap(own, "row", 2)])
-        acts = gather_acts(hidden_acts[example], pair)
-        grads = gather_grads(pair)
-        rows = kept_rows[example]
-        cols = kept_cols[example]
-        offset_col = cols % width
-        place = offset_col // LANES * GROUP_PAD + rows % GROUP_PAD
-        lane = (offset_col % LANES).reshape(devices, -1)
+        rows = kept_rows[example].reshape(devices, -1)
+        cols = kept_cols[example].reshape(devices, -1)
+        place = cols % width // LANES * GROUP_PAD + rows % GROUP_PAD
+        lane = cols % LANES
         flips = parity(rows // GROUP_PAD & my_row) ^ parity(cols // width & my_col)
-        sign = ((1 - 2 * flips).astype(jnp.float32) * NORM_SCALE).reshape(devices, -1)
+        sign = jnp.where(flips == 1, -NORM_SCALE, NORM_SCALE)
+        acts, grads, picks = gather(hidden_acts[example], out_grads[example], (place, lane, sign))
         contribution = local_contributions(
-            acts, grads, second_moment, sign_flips, place, lane, sign
+            example, hidden_acts, acts, grads, second_moment, sign_flips, *picks
         )
         received = lax.all_to_all(contribution, ("row", "col"), 0, 0, tiled=True)
         outs.append(jnp.sum(received, axis=0))

time: 77.1 us -> 71.8 us (0.931)
  waiting for transfers between devices: 19.8 us -> 13.8 us
  starting transfers between devices: 13.8 us -> 17.2 us
  blocking collectives: 17.6 us -> 14.4 us
  other arithmetic: 0.95 us -> 2.65 us
  local copies, waits for them, and re-layouts: 3.23 us -> 1.83 us
    all_to_all x1 -> x0, waiting for transfers between devices: 10.7 us -> none  [gather_acts(): return lax.all_to_all(copies, 'col', 0, 0, tiled=True)]
    ppermute x5 -> x12, starting transfers between devices: 8.36 us -> 17.2 us  [swap(): lax.ppermute(x, axis, [(i, i ^ mask) for i in range(lax.axis_size(axis))])]
    all_to_all x1 -> x0, starting transfers between devices: 5.48 us -> none  [gather_acts(): return lax.all_to_all(copies, 'col', 0, 0, tiled=True)]
    ppermute x5 -> x12, waiting for transfers between devices: 9.1 us -> 13.8 us  [swap(): lax.ppermute(x, axis, [(i, i ^ mask) for i in range(lax.axis_size(axis))])]
    all_to_all x1, blocking collectives: 17.6 us -> 14.4 us  [shards(): received = lax.all_to_all(contribution, ('row', 'col'), 0, 0, tiled=True)]
    broadcast_in_dim x1 -> x0, local copies, waits for them, and re-layouts: 2.31 us -> none  [gather_acts(): copies = jnp.broadcast_to(x[None], (peers,) + x.shape)]
    select_n x1 -> x2, other arithmetic: 0.05 us -> 1.99 us  [the longest x1 1.01 us: shards(): sign = jnp.where(flips == 1, -NORM_SCALE, NORM_SCALE)]
    unnamed x8 -> x5, local copies, waits for them, and re-layouts: 0.92 us -> 1.81 us
  transfers between devices with their start and end apart: 6 -> 12, of which waited for: 6 -> 7; matrix products, arithmetic and copies ran while one was open for 2% -> 4% of each run, Pallas kernels for 0% -> 0%
where the time goes in v4:
time: 71.8 us; the launch traced here: 70.9 us
  Pallas kernels  21 us (29%)
  starting transfers between devices  17.2 us (24%)
  blocking collectives  14.4 us (20%)
  waiting for transfers between devices  13.8 us (19%)
  other arithmetic  2.65 us (4%)
  local copies, waits for them, and re-layouts  1.83 us (3%)
    pallas_call x1, Pallas kernels, local_contributions(): pl.pallas_call(functools.partial(local_kernel, example, acts_masks, grads...  21 us
    ppermute x12, starting transfers between devices, swap(): lax.ppermute(x, axis, [(i, i ^ mask) for i in range(lax.axis_size(axis))])  17.2 us
    all_to_all x1, blocking collectives, shards(): received = lax.all_to_all(contribution, ('row', 'col'), 0, 0, tiled=True)  14.4 us
    ppermute x12, waiting for transfers between devices, swap(): lax.ppermute(x, axis, [(i, i ^ mask) for i in range(lax.axis_size(axis))])  13.8 us
    unnamed x5, local copies, waits for them, and re-layouts  1.81 us
  transfers between devices with their start and end apart: 12, of which 7 were waited for; matrix products, arithmetic and copies ran while one was open for 4% of the time, Pallas kernels for 0%

profile of v4, /device:TPU:0, one launch (start us, length us, event | category | flops | bytes accessed | tf_op | source)
XLA Modules:
  0.0 70.9 jit_solution(14718863091233316509)
XLA Ops:
  0.0 1.7 %collective-permute-start = (bf16[1,64,1792]{2,1,0:T(8,128)(2,1)}, bf16[1,64,1792]{2,1,0:T(8,128)(2,1)S(1)}, u32[]{:S(2)}, u32[]{:S(2)}) collective-permute-start(bf16[1,64,1792]{2,1,0:T(8,128)(2,1)} %own_acts.1), channel_id=1, source_target_pairs={{0,1},{1,0},{2,3},{3,2},{4,5},{5,4},{6,7},{7,6},{8,9},{9,8},{10,11... | collective-permute-start | bytes 688136 | tf_op jit(solution)/shard_map/ppermute | solution.py:241
  1.7 2.2 %collective-permute-start.1 = (bf16[1,64,1792]{2,1,0:T(8,128)(2,1)}, bf16[1,64,1792]{2,1,0:T(8,128)(2,1)S(1)}, u32[]{:S(2)}, u32[]{:S(2)}) collective-permute-start(bf16[1,64,1792]{2,1,0:T(8,128)(2,1)} %own_acts.1), channel_id=1, source_target_pairs={{0,3},{1,2},{2,1},{3,0},{4,7},{5,6},{6,5},{7,4},{8,11},{9,10},{10,... | collective-permute-start | bytes 688136 | tf_op jit(solution)/shard_map/ppermute | solution.py:241
  3.8 1.9 %collective-permute-start.2 = (bf16[1,64,1792]{2,1,0:T(8,128)(2,1)}, bf16[1,64,1792]{2,1,0:T(8,128)(2,1)S(1)}, u32[]{:S(2)}, u32[]{:S(2)}) collective-permute-start(bf16[1,64,1792]{2,1,0:T(8,128)(2,1)} %own_acts.1), channel_id=1, source_target_pairs={{0,4},{1,5},{2,6},{3,7},{4,0},{5,1},{6,2},{7,3},{8,12},{9,13},{10,... | collective-permute-start | bytes 688136 | tf_op jit(solution)/shard_map/ppermute | solution.py:241
  5.8 3.6 %collective-permute-start.3 = (bf16[1,32,1024]{2,1,0:T(8,128)(2,1)}, bf16[1,32,1024]{2,1,0:T(8,128)(2,1)S(1)}, u32[]{:S(2)}, u32[]{:S(2)}) collective-permute-start(bf16[1,32,1024]{2,1,0:T(8,128)(2,1)} %param.7), channel_id=1, source_target_pairs={{0,16},{8,24},{16,0},{24,8},{32,48},{40,56},{48,32},{56,40},{64,80... | collective-permute-start | bytes 196616 | tf_op jit(solution)/shard_map/ppermute | solution.py:241
  9.3 1.0 %add_select_fusion.2 = (s32[128,128]{1,0:T(8,128)S(1)}, s32[128,128]{1,0:T(8,128)S(1)}) fusion(s32[128,128]{1,0:T(8,128)} %bitcast.7, s32[128,128]{1,0:T(8,128)} %bitcast.9), kind=kLoop, calls=%fused_computation.12 | loop fusion | flops 770048 | bytes 262144 | tf_op jit(solution)/shard_map/jit(remainder)/select_n | solution.py:276
  10.3 1.0 %compare_select_fusion.sign_ref = f32[128,128]{1,0:T(8,128)S(1)} fusion(s32[128,128]{1,0:T(8,128)} %bitcast.8, s32[128,128]{1,0:T(8,128)} %bitcast.10, s32[]{:T(128)S(6)} %axis_index.25, s32[]{:T(128)S(6)} %axis_index.23), kind=kLoop, calls=%fused_computation.38 | loop fusion | flops 868352 | bytes 196616 | tf_op jit(solution)/shard_map/jit(_where)/select_n | solution.py:278
  11.3 0.9 %constant_dynamic-update-slice_fusion.1 = (bf16[2,32,1024]{2,1,0:T(8,128)(2,1)S(1)}, bf16[8,32,1024]{2,1,0:T(8,128)(2,1)S(1)}) fusion(bf16[1,32,1024]{2,1,0:T(8,128)(2,1)} %param.7), kind=kLoop, calls=%fused_computation.42 | loop fusion | bytes 196608
  12.2 3.5 %collective-permute-done.3 = bf16[1,32,1024]{2,1,0:T(8,128)(2,1)S(1)} collective-permute-done((bf16[1,32,1024]{2,1,0:T(8,128)(2,1)}, bf16[1,32,1024]{2,1,0:T(8,128)(2,1)S(1)}, u32[]{:S(2)}, u32[]{:S(2)}) %collective-permute-start.3) | collective-permute-done | bytes 65568 | tf_op jit(solution)/shard_map/ppermute | solution.py:241
  15.7 0.0 collective-permute-done.rest_0_
  15.7 0.0 collective-permute-done.1.rest_2_
  15.7 0.0 collective-permute-done.2.rest_3_
  15.7 1.6 %collective-permute-start.8 = (bf16[2,32,1024]{2,1,0:T(8,128)(2,1)S(1)}, bf16[2,32,1024]{2,1,0:T(8,128)(2,1)S(1)}, u32[]{:S(2)}, u32[]{:S(2)}) collective-permute-start(bf16[2,32,1024]{2,1,0:T(8,128)(2,1)S(1)} %get-tuple-element.35), channel_id=1, source_target_pairs={{0,32},{8,40},{16,48},{24,56},{32,0},{40,8},{48,16},{56,24},{64,96... | collective-permute-start | bytes 393224 | tf_op jit(solution)/shard_map/ppermute | solution.py:241
  17.3 2.1 %collective-permute-start.9 = (bf16[2,32,1024]{2,1,0:T(8,128)(2,1)S(1)}, bf16[2,32,1024]{2,1,0:T(8,128)(2,1)S(1)}, u32[]{:S(2)}, u32[]{:S(2)}) collective-permute-start(bf16[2,32,1024]{2,1,0:T(8,128)(2,1)S(1)} %get-tuple-element.35), channel_id=1, source_target_pairs={{0,96},{8,104},{16,112},{24,120},{32,64},{40,72},{48,80},{56,88},{... | collective-permute-start | bytes 393224 | tf_op jit(solution)/shard_map/ppermute | solution.py:241
  19.4 0.2 collective-permute-start.6
  19.7 0.6 collective-permute-start.10
  20.3 2.3 %collective-permute-start.4 = (bf16[1,64,1792]{2,1,0:T(8,128)(2,1)S(1)}, bf16[1,64,1792]{2,1,0:T(8,128)(2,1)S(1)}, u32[]{:S(2)}, u32[]{:S(2)}) collective-permute-start(bf16[1,64,1792]{2,1,0:T(8,128)(2,1)S(1)} %collective-permute-done.rest_0_), channel_id=1, source_target_pairs={{0,3},{1,2},{2,1},{3,0},{4,7},{5,6},{6,5},{7,4},{8,11},{9,10},{10,... | collective-permute-start | bytes 688136 | tf_op jit(solution)/shard_map/ppermute | solution.py:241
  22.6 0.0 collective-permute-done.8
  22.6 0.1 collective-permute-start.5
  22.8 1.5 %collective-permute-done.9 = bf16[2,32,1024]{2,1,0:T(8,128)(2,1)S(1)} collective-permute-done((bf16[2,32,1024]{2,1,0:T(8,128)(2,1)S(1)}, bf16[2,32,1024]{2,1,0:T(8,128)(2,1)S(1)}, u32[]{:S(2)}, u32[]{:S(2)}) %collective-permute-start.9) | collective-permute-done | bytes 131104 | tf_op jit(solution)/shard_map/ppermute | solution.py:241
  24.3 0.8 %collective-permute-start.7 = (bf16[1,64,1792]{2,1,0:T(8,128)(2,1)S(1)}, bf16[1,64,1792]{2,1,0:T(8,128)(2,1)S(1)}, u32[]{:S(2)}, u32[]{:S(2)}) collective-permute-start(bf16[1,64,1792]{2,1,0:T(8,128)(2,1)S(1)} %collective-permute-done.1.rest_2_), channel_id=1, source_target_pairs={{0,4},{1,5},{2,6},{3,7},{4,0},{5,1},{6,2},{7,3},{8,12},{9,13},{10,... | collective-permute-start | bytes 688136 | tf_op jit(solution)/shard_map/ppermute | solution.py:241
  25.1 1.0 %collective-permute-done.10 = bf16[2,32,1024]{2,1,0:T(8,128)(2,1)S(1)} collective-permute-done((bf16[2,32,1024]{2,1,0:T(8,128)(2,1)S(1)}, bf16[2,32,1024]{2,1,0:T(8,128)(2,1)S(1)}, u32[]{:S(2)}, u32[]{:S(2)}) %collective-permute-start.10) | collective-permute-done | bytes 131104 | tf_op jit(solution)/shard_map/ppermute | solution.py:241
  26.1 3.5 %collective-permute-done.6.rest_5_ = bf16[1,64,1792]{2,1,0:T(8,128)(2,1)S(1)} collective-permute-done((bf16[1,64,1792]{2,1,0:T(8,128)(2,1)}, bf16[1,64,1792]{2,1,0:T(8,128)(2,1)S(1)}, u32[]{:S(2)}, u32[]{:S(2)}) %collective-permute-start.6) | collective-permute-done | bytes 229408 | tf_op jit(solution)/shard_map/ppermute | solution.py:241
  29.6 0.7 collective-permute-done.4.rest_1_
  30.3 0.0 collective-permute-done.5.rest_4_
  30.3 1.7 %collective-permute-done.7.rest_6_ = bf16[1,64,1792]{2,1,0:T(8,128)(2,1)S(1)} collective-permute-done((bf16[1,64,1792]{2,1,0:T(8,128)(2,1)S(1)}, bf16[1,64,1792]{2,1,0:T(8,128)(2,1)S(1)}, u32[]{:S(2)}, u32[]{:S(2)}) %collective-permute-start.7) | collective-permute-done | bytes 229408 | tf_op jit(solution)/shard_map/ppermute | solution.py:241
  31.9 0.0 collective-permute-start.11
  32.0 1.9 %collective-permute-done.11.rest_8_ = bf16[8,32,1024]{2,1,0:T(8,128)(2,1)S(1)} collective-permute-done((bf16[8,32,1024]{2,1,0:T(8,128)(2,1)S(1)}, bf16[8,32,1024]{2,1,0:T(8,128)(2,1)S(1)}, u32[]{:S(2)}, u32[]{:S(2)}) %collective-permute-start.11) | collective-permute-done | bytes 524320 | tf_op jit(solution)/shard_map/ppermute | solution.py:241
  33.9 0.0 copy-start
  33.9 0.9 %copy-done = bf16[1,64,1792]{2,1,0:T(8,128)(2,1)S(1)} copy-done((bf16[1,64,1792]{2,1,0:T(8,128)(2,1)S(1)}, bf16[1,64,1792]{2,1,0:T(8,128)(2,1)}, u32[]{:S(2)}) %copy-start) | copy-done | bytes 229400
  34.8 21.0 %shard_map.64 = f32[128,128]{1,0:T(8,128)S(1)} custom-call(bf16[1,64,1792]{2,1,0:T(8,128)(2,1)S(1)} %copy-done, f32[1792,1024]{1,0:T(8,128)} %moment_ref.1, bf16[1792,1024]{1,0:T(8,128)(2,1)} %flips_ref.1, s32[128,128]{1,0:T(8,128)S(1)} %get-tuple-element.20.place_ref, s32[128,128]{1,0:T(8,128)S(1)} %get-tuple-element.21.lane_ref, ...), custom_call_target="tpu_custom_call" | custom-call | tf_op jit(solution)/shard_map/pallas_call | solution.py:216
  55.8 14.4 %all_to_all.9 = f32[128,1,128]{2,1,0:T(1,128)S(1)} all-to-all(f32[128,1,128]{2,1,0:T(1,128)S(1)} %bitcast.6), channel_id=1, replica_groups=mesh['row'=16,'col'=8] {'row','col'}, dimensions={0} | all-to-all | bytes 131072 | tf_op jit(solution)/shard_map/all_to_all | solution.py:283
  70.2 0.7 reduce_sum.9
  (4 shorter events, 0.0 us)
Async XLA Ops:
  0.0 15.7 %collective-permute-start = (bf16[1,64,1792]{2,1,0:T(8,128)(2,1)}, bf16[1,64,1792]{2,1,0:T(8,128)(2,1)S(1)}, u32[]{:S(2)}, u32[]{:S(2)}) collective-permute-start(bf16[1,64,1792]{2,1,0:T(8,128)(2,1)} %own_acts.1), channel_id=1, source_target_pairs={{0,1},{1,0},{2,3},{3,2},{4,5},{5,4},{6,7},{7,6},{8,9},{9,8},{10,11... | collective-permute-start | bytes 688136 | tf_op jit(solution)/shard_map/ppermute | solution.py:241
  1.7 14.1 %collective-permute-start.1 = (bf16[1,64,1792]{2,1,0:T(8,128)(2,1)}, bf16[1,64,1792]{2,1,0:T(8,128)(2,1)S(1)}, u32[]{:S(2)}, u32[]{:S(2)}) collective-permute-start(bf16[1,64,1792]{2,1,0:T(8,128)(2,1)} %own_acts.1), channel_id=1, source_target_pairs={{0,3},{1,2},{2,1},{3,0},{4,7},{5,6},{6,5},{7,4},{8,11},{9,10},{10,... | collective-permute-start | bytes 688136 | tf_op jit(solution)/shard_map/ppermute | solution.py:241
  3.8 11.9 %collective-permute-start.2 = (bf16[1,64,1792]{2,1,0:T(8,128)(2,1)}, bf16[1,64,1792]{2,1,0:T(8,128)(2,1)S(1)}, u32[]{:S(2)}, u32[]{:S(2)}) collective-permute-start(bf16[1,64,1792]{2,1,0:T(8,128)(2,1)} %own_acts.1), channel_id=1, source_target_pairs={{0,4},{1,5},{2,6},{3,7},{4,0},{5,1},{6,2},{7,3},{8,12},{9,13},{10,... | collective-permute-start | bytes 688136 | tf_op jit(solution)/shard_map/ppermute | solution.py:241
  5.8 10.0 %collective-permute-start.3 = (bf16[1,32,1024]{2,1,0:T(8,128)(2,1)}, bf16[1,32,1024]{2,1,0:T(8,128)(2,1)S(1)}, u32[]{:S(2)}, u32[]{:S(2)}) collective-permute-start(bf16[1,32,1024]{2,1,0:T(8,128)(2,1)} %param.7), channel_id=1, source_target_pairs={{0,16},{8,24},{16,0},{24,8},{32,48},{40,56},{48,32},{56,40},{64,80... | collective-permute-start | bytes 196616 | tf_op jit(solution)/shard_map/ppermute | solution.py:241
  15.7 6.9 %collective-permute-start.8 = (bf16[2,32,1024]{2,1,0:T(8,128)(2,1)S(1)}, bf16[2,32,1024]{2,1,0:T(8,128)(2,1)S(1)}, u32[]{:S(2)}, u32[]{:S(2)}) collective-permute-start(bf16[2,32,1024]{2,1,0:T(8,128)(2,1)S(1)} %get-tuple-element.35), channel_id=1, source_target_pairs={{0,32},{8,40},{16,48},{24,56},{32,0},{40,8},{48,16},{56,24},{64,96... | collective-permute-start | bytes 393224 | tf_op jit(solution)/shard_map/ppermute | solution.py:241
  17.3 7.0 %collective-permute-start.9 = (bf16[2,32,1024]{2,1,0:T(8,128)(2,1)S(1)}, bf16[2,32,1024]{2,1,0:T(8,128)(2,1)S(1)}, u32[]{:S(2)}, u32[]{:S(2)}) collective-permute-start(bf16[2,32,1024]{2,1,0:T(8,128)(2,1)S(1)} %get-tuple-element.35), channel_id=1, source_target_pairs={{0,96},{8,104},{16,112},{24,120},{32,64},{40,72},{48,80},{56,88},{... | collective-permute-start | bytes 393224 | tf_op jit(solution)/shard_map/ppermute | solution.py:241
  19.4 10.2 %collective-permute-start.6 = (bf16[1,64,1792]{2,1,0:T(8,128)(2,1)}, bf16[1,64,1792]{2,1,0:T(8,128)(2,1)S(1)}, u32[]{:S(2)}, u32[]{:S(2)}) collective-permute-start(bf16[1,64,1792]{2,1,0:T(8,128)(2,1)} %own_acts.1), channel_id=1, source_target_pairs={{0,6},{1,7},{2,4},{3,5},{4,2},{5,3},{6,0},{7,1},{8,14},{9,15},{10,... | collective-permute-start | bytes 688136 | tf_op jit(solution)/shard_map/ppermute | solution.py:241
  19.7 6.5 %collective-permute-start.10 = (bf16[2,32,1024]{2,1,0:T(8,128)(2,1)S(1)}, bf16[2,32,1024]{2,1,0:T(8,128)(2,1)S(1)}, u32[]{:S(2)}, u32[]{:S(2)}) collective-permute-start(bf16[2,32,1024]{2,1,0:T(8,128)(2,1)S(1)} %get-tuple-element.35), channel_id=1, source_target_pairs={{0,64},{8,72},{16,80},{24,88},{32,96},{40,104},{48,112},{56,120},{... | collective-permute-start | bytes 393224 | tf_op jit(solution)/shard_map/ppermute | solution.py:241
  20.3 10.0 %collective-permute-start.4 = (bf16[1,64,1792]{2,1,0:T(8,128)(2,1)S(1)}, bf16[1,64,1792]{2,1,0:T(8,128)(2,1)S(1)}, u32[]{:S(2)}, u32[]{:S(2)}) collective-permute-start(bf16[1,64,1792]{2,1,0:T(8,128)(2,1)S(1)} %collective-permute-done.rest_0_), channel_id=1, source_target_pairs={{0,3},{1,2},{2,1},{3,0},{4,7},{5,6},{6,5},{7,4},{8,11},{9,10},{10,... | collective-permute-start | bytes 688136 | tf_op jit(solution)/shard_map/ppermute | solution.py:241
  22.6 7.6 %collective-permute-start.5 = (bf16[1,64,1792]{2,1,0:T(8,128)(2,1)S(1)}, bf16[1,64,1792]{2,1,0:T(8,128)(2,1)S(1)}, u32[]{:S(2)}, u32[]{:S(2)}) collective-permute-start(bf16[1,64,1792]{2,1,0:T(8,128)(2,1)S(1)} %collective-permute-done.2.rest_3_), channel_id=1, source_target_pairs={{0,1},{1,0},{2,3},{3,2},{4,5},{5,4},{6,7},{7,6},{8,9},{9,8},{10,11... | collective-permute-start | bytes 688136 | tf_op jit(solution)/shard_map/ppermute | solution.py:241
  24.3 7.6 %collective-permute-start.7 = (bf16[1,64,1792]{2,1,0:T(8,128)(2,1)S(1)}, bf16[1,64,1792]{2,1,0:T(8,128)(2,1)S(1)}, u32[]{:S(2)}, u32[]{:S(2)}) collective-permute-start(bf16[1,64,1792]{2,1,0:T(8,128)(2,1)S(1)} %collective-permute-done.1.rest_2_), channel_id=1, source_target_pairs={{0,4},{1,5},{2,6},{3,7},{4,0},{5,1},{6,2},{7,3},{8,12},{9,13},{10,... | collective-permute-start | bytes 688136 | tf_op jit(solution)/shard_map/ppermute | solution.py:241
  31.9 1.9 %collective-permute-start.11 = (bf16[8,32,1024]{2,1,0:T(8,128)(2,1)S(1)}, bf16[8,32,1024]{2,1,0:T(8,128)(2,1)S(1)}, u32[]{:S(2)}, u32[]{:S(2)}) collective-permute-start(bf16[8,32,1024]{2,1,0:T(8,128)(2,1)S(1)} %constant_dynamic-update-slice_fusion.2.rest_7_), channel_id=1, source_target_pairs={{0,8},{8,0},{16,24},{24,16},{32,40},{40,32},{48,56},{56,48},{64,72... | collective-permute-start | bytes 1572872 | tf_op jit(solution)/shard_map/ppermute | solution.py:241
  33.9 0.9 %copy-start = (bf16[1,64,1792]{2,1,0:T(8,128)(2,1)S(1)}, bf16[1,64,1792]{2,1,0:T(8,128)(2,1)}, u32[]{:S(2)}) copy-start(bf16[1,64,1792]{2,1,0:T(8,128)(2,1)} %own_acts.1) | copy-start | bytes 688132

commit v5 on v4

--- a/solution.py
+++ b/solution.py
@@ -19,7 +19,8 @@
 SUBLANES = 8
 TILE = 256
 CHUNK = 64
-PLACE_SLOTS = 4
+PLACE_SLOTS = 2
+PLACE_ROWS = 32
 
 
 def parity(values):
@@ -57,18 +58,17 @@
 
 
 def local_kernel(
-    example, acts_masks, grads_masks, own_acts, moment_ref, flips_ref, place_ref, lane_ref, sign_ref, *rest
+    acts_masks, grads_masks, moment_ref, flips_ref, place_ref, lane_ref, sign_ref, *rest
 ):
     acts_pieces, rest = rest[: len(acts_masks)], rest[len(acts_masks) :]
     grads_pieces, rest = rest[: len(grads_masks)], rest[len(grads_masks) :]
     out_ref, acts_ref, grads_ref, moment, flips, scaled, half, inner, whole, *rest = rest
-    own_sem, *rest = rest
     *places, moment_sem, flips_sem, place_sem = rest
     hidden, width = inner.shape
     blocks = hidden // TILE
     padded_blocks = GROUP_PAD // TILE
     strips = width // TILE
-    groups = out_ref.shape[0] // SUBLANES
+    groups = out_ref.shape[0] // PLACE_ROWS
 
     def block_copies(block):
         rows = pl.ds(pl.multiple_of(block * TILE, TILE), TILE)
@@ -82,18 +82,11 @@
 
     def place_copy(group, slot):
         return pltpu.make_async_copy(
-            place_ref.at[pl.ds(pl.multiple_of(group * SUBLANES, SUBLANES), SUBLANES), :],
+            place_ref.at[pl.ds(pl.multiple_of(group * PLACE_ROWS, PLACE_ROWS), PLACE_ROWS), :],
             places[slot],
             place_sem.at[slot],
         )
 
-
-    own_tokens = own_acts.shape[1]
-    own_start = pl.multiple_of(lax.axis_index("col") * own_tokens, own_tokens)
-    own_copy = pltpu.make_async_copy(
-        own_acts.at[example], acts_ref.at[pl.ds(own_start, own_tokens), :], own_sem
-    )
-    own_copy.start()
     for block in range(blocks):
         for copy in block_copies(block):
             copy.start()
@@ -109,7 +102,6 @@
             for number, mask in enumerate(piece_masks):
                 start = pl.multiple_of((mine ^ mask) * tokens, tokens)
                 target[pl.ds(start, tokens), :] = piece[number]
-    own_copy.wait()
 
     matrix = sylvester(TILE)
     matrix_beside = jnp.concatenate([matrix, matrix], axis=1)
@@ -189,34 +181,36 @@
         for slot, place in enumerate(places):
             group = step * len(places) + slot
             place_copy(group, slot).wait()
-            rows = pl.ds(pl.multiple_of(group * SUBLANES, SUBLANES), SUBLANES)
-            lanes = lane_ref[rows, :]
-            picked = jnp.zeros((SUBLANES, LANES), jnp.float32)
-            for lane in range(LANES):
-                held = None
-                for sublane in range(SUBLANES):
-                    row = whole[pl.ds(place[sublane, lane], 1), :]
-                    row = jnp.broadcast_to(row, (SUBLANES, LANES))
-                    held = row if held is None else jnp.where(sublane_ids == sublane, row, held)
-                picked = jnp.where(lane_ids == lane, jnp.take_along_axis(held, lanes, axis=1), picked)
-            out_ref[rows, :] = picked * sign_ref[rows, :]
+            for part in range(0, PLACE_ROWS, SUBLANES):
+                rows = pl.ds(pl.multiple_of(group * PLACE_ROWS + part, SUBLANES), SUBLANES)
+                lanes = lane_ref[rows, :]
+                picked = jnp.zeros((SUBLANES, LANES), jnp.float32)
+                for lane in range(LANES):
+                    held = None
+                    for sublane in range(SUBLANES):
+                        row = whole[pl.ds(place[part + sublane, lane], 1), :]
+                        row = jnp.broadcast_to(row, (SUBLANES, LANES))
+                        held = row if held is None else jnp.where(sublane_ids == sublane, row, held)
+                    held = jnp.take_along_axis(held, lanes, axis=1)
+                    picked = jnp.where(lane_ids == lane, held, picked)
+                out_ref[rows, :] = picked * sign_ref[rows, :]
 
             @pl.when(group + len(places) < groups)
             def _():
                 place_copy(group + len(places), slot).start()
 
 
-def local_contributions(example, hidden_acts, acts, grads, moment, flips, place, lane, sign):
+def local_contributions(acts, grads, moment, flips, place, lane, sign):
     hidden, width = moment.shape
     acts_masks, acts = zip(*acts)
     grads_masks, grads = zip(*grads)
-    tokens = hidden_acts.shape[1] + sum(x.shape[0] * x.shape[1] for x in acts)
+    tokens = sum(len(own) * x.shape[1] for own, x in zip(grads_masks, grads))
     in_vmem = pl.BlockSpec(memory_space=pltpu.VMEM)
     in_hbm = pl.BlockSpec(memory_space=pltpu.HBM)
     return pl.pallas_call(
-        functools.partial(local_kernel, example, acts_masks, grads_masks),
+        functools.partial(local_kernel, acts_masks, grads_masks),
         out_shape=jax.ShapeDtypeStruct(place.shape, jnp.float32),
-        in_specs=[in_hbm] * 3 + [in_vmem] * (3 +  len(acts) + len(grads)),
+        in_specs=[in_hbm] * 2 + [in_vmem] * (3 + len(acts) + len(grads)),
         out_specs=in_vmem,
         scratch_shapes=[
             pltpu.VMEM((tokens, hidden), jnp.bfloat16),
@@ -227,14 +221,13 @@
             pltpu.VMEM((2 * TILE, width), jnp.bfloat16),
             pltpu.VMEM((hidden, width), jnp.float32),
             pltpu.VMEM((width // LANES * GROUP_PAD, LANES), jnp.float32),
-            pltpu.SemaphoreType.DMA(()),
-            *[pltpu.SMEM((SUBLANES, LANES), jnp.int32)] * PLACE_SLOTS,
+            *[pltpu.SMEM((PLACE_ROWS, LANES), jnp.int32)] * PLACE_SLOTS,
             pltpu.SemaphoreType.DMA((hidden // TILE,)),
             pltpu.SemaphoreType.DMA((hidden // TILE,)),
             pltpu.SemaphoreType.DMA((PLACE_SLOTS,)),
         ],
         compiler_params=pltpu.CompilerParams(vmem_limit_bytes=48 * 2**20),
-    )(hidden_acts, moment, flips, place, lane, sign, *acts, *grads)
+    )(moment, flips, place, lane, sign, *acts, *grads)
 
 
 def swap(x, axis, mask):
@@ -248,7 +241,8 @@
     for mask in (4, 1, 3):
         held[mask] = swap(held[0], "col", mask)
     far = swap(held[0], "col", 6)
-    held, near, meanwhile = lax.optimization_barrier((held, near, meanwhile))
+    mine = jnp.pad(held[0], ((0, 1), (0, 0), (0, 0)))
+    held, near, mine, meanwhile = lax.optimization_barrier((held, near, mine, meanwhile))
     held[5] = swap(held[4], "col", 1)
     held[2] = swap(held[1], "col", 3)
     held[7] = swap(held[3], "col", 4)
@@ -257,7 +251,7 @@
     half = jnp.concatenate([pair] + [swap(pair, "row", mask) for mask in (4, 12, 8)])
     held, half = lax.optimization_barrier((held, half))
     other = swap(half, "row", 1)
-    acts = [((mask,), piece) for mask, piece in held.items() if mask]
+    acts = [((mask,), piece) for mask, piece in held.items() if mask] + [((0,), mine)]
     masks = tuple(far ^ near for far in (0, 4, 12, 8) for near in (0, 2))
     return acts, [(masks, half), (tuple(mask ^ 1 for mask in masks), other)], meanwhile
 
@@ -277,9 +271,7 @@
         flips = parity(rows // GROUP_PAD & my_row) ^ parity(cols // width & my_col)
         sign = jnp.where(flips == 1, -NORM_SCALE, NORM_SCALE)
         acts, grads, picks = gather(hidden_acts[example], out_grads[example], (place, lane, sign))
-        contribution = local_contributions(
-            example, hidden_acts, acts, grads, second_moment, sign_flips, *picks
-        )
+        contribution = local_contributions(acts, grads, second_moment, sign_flips, *picks)
         received = lax.all_to_all(contribution, ("row", "col"), 0, 0, tiled=True)
         outs.append(jnp.sum(received, axis=0))
     return jnp.stack(outs)

time: 71.8 us -> 69.6 us (0.969)
  Pallas kernels: 21 us -> 19.6 us
  waiting for transfers between devices: 13.8 us -> 12.8 us
    pallas_call x1, Pallas kernels: 21 us -> 19.6 us  [local_contributions(): pl.pallas_call(functools.partial(local_kernel, acts_masks, grads_masks),...]
    ppermute x12, waiting for transfers between devices: 13.8 us -> 12.8 us  [swap(): lax.ppermute(x, axis, [(i, i ^ mask) for i in range(lax.axis_size(axis))])]
    pad x0 -> x1, local copies, waits for them, and re-layouts: none -> 0.97 us  [gather(): mine = jnp.pad(held[0], ((0, 1), (0, 0), (0, 0)))]
    unnamed x5 -> x3, local copies, waits for them, and re-layouts: 1.81 us -> 0.87 us
  transfers between devices with their start and end apart: 12 -> 12, of which waited for: 7 -> 7; matrix products, arithmetic and copies ran while one was open for 4% -> 6% of each run, Pallas kernels for 0% -> 0%
where the time goes in v5:
time: 69.6 us; the launch traced here: 68.6 us
  Pallas kernels  19.6 us (28%)
  starting transfers between devices  17.2 us (25%)
  blocking collectives  14.4 us (21%)
  waiting for transfers between devices  12.8 us (18%)
  other arithmetic  2.65 us (4%)
  local copies, waits for them, and re-layouts  1.86 us (3%)
    pallas_call x1, Pallas kernels, local_contributions(): pl.pallas_call(functools.partial(local_kernel, acts_masks, grads_masks),...  19.6 us
    ppermute x12, starting transfers between devices, swap(): lax.ppermute(x, axis, [(i, i ^ mask) for i in range(lax.axis_size(axis))])  17.2 us
    all_to_all x1, blocking collectives, shards(): received = lax.all_to_all(contribution, ('row', 'col'), 0, 0, tiled=True)  14.4 us
    ppermute x12, waiting for transfers between devices, swap(): lax.ppermute(x, axis, [(i, i ^ mask) for i in range(lax.axis_size(axis))])  12.8 us
  transfers between devices with their start and end apart: 12, of which 7 were waited for; matrix products, arithmetic and copies ran while one was open for 6% of the time, Pallas kernels for 0%

profile of v5, /device:TPU:0, one launch (start us, length us, event | category | flops | bytes accessed | tf_op | source)
XLA Modules:
  0.0 68.6 jit_solution(17462251381089212531)
XLA Ops:
  0.0 1.7 %collective-permute-start = (bf16[1,64,1792]{2,1,0:T(8,128)(2,1)}, bf16[1,64,1792]{2,1,0:T(8,128)(2,1)S(1)}, u32[]{:S(2)}, u32[]{:S(2)}) collective-permute-start(bf16[1,64,1792]{2,1,0:T(8,128)(2,1)} %param.6), channel_id=1, source_target_pairs={{0,1},{1,0},{2,3},{3,2},{4,5},{5,4},{6,7},{7,6},{8,9},{9,8},{10,11... | collective-permute-start | bytes 688136 | tf_op jit(solution)/shard_map/ppermute | solution.py:234
  1.7 2.2 %collective-permute-start.1 = (bf16[1,64,1792]{2,1,0:T(8,128)(2,1)}, bf16[1,64,1792]{2,1,0:T(8,128)(2,1)S(1)}, u32[]{:S(2)}, u32[]{:S(2)}) collective-permute-start(bf16[1,64,1792]{2,1,0:T(8,128)(2,1)} %param.6), channel_id=1, source_target_pairs={{0,3},{1,2},{2,1},{3,0},{4,7},{5,6},{6,5},{7,4},{8,11},{9,10},{10,... | collective-permute-start | bytes 688136 | tf_op jit(solution)/shard_map/ppermute | solution.py:234
  3.8 1.9 %collective-permute-start.2 = (bf16[1,64,1792]{2,1,0:T(8,128)(2,1)}, bf16[1,64,1792]{2,1,0:T(8,128)(2,1)S(1)}, u32[]{:S(2)}, u32[]{:S(2)}) collective-permute-start(bf16[1,64,1792]{2,1,0:T(8,128)(2,1)} %param.6), channel_id=1, source_target_pairs={{0,4},{1,5},{2,6},{3,7},{4,0},{5,1},{6,2},{7,3},{8,12},{9,13},{10,... | collective-permute-start | bytes 688136 | tf_op jit(solution)/shard_map/ppermute | solution.py:234
  5.8 3.6 %collective-permute-start.3 = (bf16[1,32,1024]{2,1,0:T(8,128)(2,1)}, bf16[1,32,1024]{2,1,0:T(8,128)(2,1)S(1)}, u32[]{:S(2)}, u32[]{:S(2)}) collective-permute-start(bf16[1,32,1024]{2,1,0:T(8,128)(2,1)} %param.7), channel_id=1, source_target_pairs={{0,16},{8,24},{16,0},{24,8},{32,48},{40,56},{48,32},{56,40},{64,80... | collective-permute-start | bytes 196616 | tf_op jit(solution)/shard_map/ppermute | solution.py:234
  9.3 1.0 %add_select_fusion.2 = (s32[128,128]{1,0:T(8,128)S(1)}, s32[128,128]{1,0:T(8,128)S(1)}) fusion(s32[128,128]{1,0:T(8,128)} %bitcast.7, s32[128,128]{1,0:T(8,128)} %bitcast.9), kind=kLoop, calls=%fused_computation.12 | loop fusion | flops 770048 | bytes 262144 | tf_op jit(solution)/shard_map/jit(remainder)/select_n | solution.py:270
  10.3 1.0 %compare_select_fusion.sign_ref = f32[128,128]{1,0:T(8,128)S(1)} fusion(s32[128,128]{1,0:T(8,128)} %bitcast.8, s32[128,128]{1,0:T(8,128)} %bitcast.10, s32[]{:T(128)S(6)} %axis_index.25, s32[]{:T(128)S(6)} %axis_index.23), kind=kLoop, calls=%fused_computation.38 | loop fusion | flops 868352 | bytes 196616 | tf_op jit(solution)/shard_map/jit(_where)/select_n | solution.py:272
  11.3 1.0 %pad.4.rest_7_ = bf16[2,64,1792]{2,1,0:T(8,128)(2,1)S(1)} pad(bf16[1,64,1792]{2,1,0:T(8,128)(2,1)} %param.6, bf16[]{:T(256)} %constant.72.clone.1), padding=0_1x0_0x0_0 | pad | bytes 688130 | tf_op jit(solution)/shard_map/jit(_pad)/pad | solution.py:244
  12.3 0.9 %constant_dynamic-update-slice_fusion.1 = (bf16[2,32,1024]{2,1,0:T(8,128)(2,1)S(1)}, bf16[8,32,1024]{2,1,0:T(8,128)(2,1)S(1)}) fusion(bf16[1,32,1024]{2,1,0:T(8,128)(2,1)} %param.7), kind=kLoop, calls=%fused_computation.42 | loop fusion | bytes 196608
  13.2 2.6 %collective-permute-done.3 = bf16[1,32,1024]{2,1,0:T(8,128)(2,1)S(1)} collective-permute-done((bf16[1,32,1024]{2,1,0:T(8,128)(2,1)}, bf16[1,32,1024]{2,1,0:T(8,128)(2,1)S(1)}, u32[]{:S(2)}, u32[]{:S(2)}) %collective-permute-start.3) | collective-permute-done | bytes 65568 | tf_op jit(solution)/shard_map/ppermute | solution.py:234
  15.7 0.0 collective-permute-done.rest_0_
  15.7 0.0 collective-permute-done.1.rest_2_
  15.7 0.0 collective-permute-done.2.rest_3_
  15.7 1.6 %collective-permute-start.8 = (bf16[2,32,1024]{2,1,0:T(8,128)(2,1)S(1)}, bf16[2,32,1024]{2,1,0:T(8,128)(2,1)S(1)}, u32[]{:S(2)}, u32[]{:S(2)}) collective-permute-start(bf16[2,32,1024]{2,1,0:T(8,128)(2,1)S(1)} %get-tuple-element.37), channel_id=1, source_target_pairs={{0,32},{8,40},{16,48},{24,56},{32,0},{40,8},{48,16},{56,24},{64,96... | collective-permute-start | bytes 393224 | tf_op jit(solution)/shard_map/ppermute | solution.py:234
  17.3 2.1 %collective-permute-start.9 = (bf16[2,32,1024]{2,1,0:T(8,128)(2,1)S(1)}, bf16[2,32,1024]{2,1,0:T(8,128)(2,1)S(1)}, u32[]{:S(2)}, u32[]{:S(2)}) collective-permute-start(bf16[2,32,1024]{2,1,0:T(8,128)(2,1)S(1)} %get-tuple-element.37), channel_id=1, source_target_pairs={{0,96},{8,104},{16,112},{24,120},{32,64},{40,72},{48,80},{56,88},{... | collective-permute-start | bytes 393224 | tf_op jit(solution)/shard_map/ppermute | solution.py:234
  19.4 0.2 collective-permute-start.6
  19.7 0.6 collective-permute-start.10
  20.3 2.3 %collective-permute-start.4 = (bf16[1,64,1792]{2,1,0:T(8,128)(2,1)S(1)}, bf16[1,64,1792]{2,1,0:T(8,128)(2,1)S(1)}, u32[]{:S(2)}, u32[]{:S(2)}) collective-permute-start(bf16[1,64,1792]{2,1,0:T(8,128)(2,1)S(1)} %collective-permute-done.rest_0_), channel_id=1, source_target_pairs={{0,3},{1,2},{2,1},{3,0},{4,7},{5,6},{6,5},{7,4},{8,11},{9,10},{10,... | collective-permute-start | bytes 688136 | tf_op jit(solution)/shard_map/ppermute | solution.py:234
  22.6 0.0 collective-permute-done.8
  22.6 0.1 collective-permute-start.5
  22.8 1.5 %collective-permute-done.9 = bf16[2,32,1024]{2,1,0:T(8,128)(2,1)S(1)} collective-permute-done((bf16[2,32,1024]{2,1,0:T(8,128)(2,1)S(1)}, bf16[2,32,1024]{2,1,0:T(8,128)(2,1)S(1)}, u32[]{:S(2)}, u32[]{:S(2)}) %collective-permute-start.9) | collective-permute-done | bytes 131104 | tf_op jit(solution)/shard_map/ppermute | solution.py:234
  24.3 0.8 %collective-permute-start.7 = (bf16[1,64,1792]{2,1,0:T(8,128)(2,1)S(1)}, bf16[1,64,1792]{2,1,0:T(8,128)(2,1)S(1)}, u32[]{:S(2)}, u32[]{:S(2)}) collective-permute-start(bf16[1,64,1792]{2,1,0:T(8,128)(2,1)S(1)} %collective-permute-done.1.rest_2_), channel_id=1, source_target_pairs={{0,4},{1,5},{2,6},{3,7},{4,0},{5,1},{6,2},{7,3},{8,12},{9,13},{10,... | collective-permute-start | bytes 688136 | tf_op jit(solution)/shard_map/ppermute | solution.py:234
  25.1 1.0 %collective-permute-done.10 = bf16[2,32,1024]{2,1,0:T(8,128)(2,1)S(1)} collective-permute-done((bf16[2,32,1024]{2,1,0:T(8,128)(2,1)S(1)}, bf16[2,32,1024]{2,1,0:T(8,128)(2,1)S(1)}, u32[]{:S(2)}, u32[]{:S(2)}) %collective-permute-start.10) | collective-permute-done | bytes 131104 | tf_op jit(solution)/shard_map/ppermute | solution.py:234
  26.1 3.5 %collective-permute-done.6.rest_5_ = bf16[1,64,1792]{2,1,0:T(8,128)(2,1)S(1)} collective-permute-done((bf16[1,64,1792]{2,1,0:T(8,128)(2,1)}, bf16[1,64,1792]{2,1,0:T(8,128)(2,1)S(1)}, u32[]{:S(2)}, u32[]{:S(2)}) %collective-permute-start.6) | collective-permute-done | bytes 229408 | tf_op jit(solution)/shard_map/ppermute | solution.py:234
  29.6 0.7 collective-permute-done.4.rest_1_
  30.3 0.0 collective-permute-done.5.rest_4_
  30.3 1.7 %collective-permute-done.7.rest_6_ = bf16[1,64,1792]{2,1,0:T(8,128)(2,1)S(1)} collective-permute-done((bf16[1,64,1792]{2,1,0:T(8,128)(2,1)S(1)}, bf16[1,64,1792]{2,1,0:T(8,128)(2,1)S(1)}, u32[]{:S(2)}, u32[]{:S(2)}) %collective-permute-start.7) | collective-permute-done | bytes 229408 | tf_op jit(solution)/shard_map/ppermute | solution.py:234
  31.9 0.0 collective-permute-start.11
  32.0 1.9 %collective-permute-done.11.rest_9_ = bf16[8,32,1024]{2,1,0:T(8,128)(2,1)S(1)} collective-permute-done((bf16[8,32,1024]{2,1,0:T(8,128)(2,1)S(1)}, bf16[8,32,1024]{2,1,0:T(8,128)(2,1)S(1)}, u32[]{:S(2)}, u32[]{:S(2)}) %collective-permute-start.11) | collective-permute-done | bytes 524320 | tf_op jit(solution)/shard_map/ppermute | solution.py:234
  33.9 19.6 %shard_map.64 = f32[128,128]{1,0:T(8,128)S(1)} custom-call(f32[1792,1024]{1,0:T(8,128)} %moment_ref.1, bf16[1792,1024]{1,0:T(8,128)(2,1)} %flips_ref.1, s32[128,128]{1,0:T(8,128)S(1)} %get-tuple-element.21.place_ref, s32[128,128]{1,0:T(8,128)S(1)} %get-tuple-element.22.lane_ref, f32[128,128]{1,0:T(8,128)S(1)} %compare_select_fusion.sign_ref, ...), custom_call_target="tpu_custom_call" | custom-call | tf_op jit(solution)/shard_map/pallas_call | solution.py:210
  53.5 14.4 %all_to_all.9 = f32[128,1,128]{2,1,0:T(1,128)S(1)} all-to-all(f32[128,1,128]{2,1,0:T(1,128)S(1)} %bitcast.6), channel_id=1, replica_groups=mesh['row'=16,'col'=8] {'row','col'}, dimensions={0} | all-to-all | bytes 131072 | tf_op jit(solution)/shard_map/all_to_all | solution.py:275
  67.9 0.7 reduce_sum.9
  (4 shorter events, 0.0 us)
Async XLA Ops:
  0.0 15.7 %collective-permute-start = (bf16[1,64,1792]{2,1,0:T(8,128)(2,1)}, bf16[1,64,1792]{2,1,0:T(8,128)(2,1)S(1)}, u32[]{:S(2)}, u32[]{:S(2)}) collective-permute-start(bf16[1,64,1792]{2,1,0:T(8,128)(2,1)} %param.6), channel_id=1, source_target_pairs={{0,1},{1,0},{2,3},{3,2},{4,5},{5,4},{6,7},{7,6},{8,9},{9,8},{10,11... | collective-permute-start | bytes 688136 | tf_op jit(solution)/shard_map/ppermute | solution.py:234
  1.7 14.1 %collective-permute-start.1 = (bf16[1,64,1792]{2,1,0:T(8,128)(2,1)}, bf16[1,64,1792]{2,1,0:T(8,128)(2,1)S(1)}, u32[]{:S(2)}, u32[]{:S(2)}) collective-permute-start(bf16[1,64,1792]{2,1,0:T(8,128)(2,1)} %param.6), channel_id=1, source_target_pairs={{0,3},{1,2},{2,1},{3,0},{4,7},{5,6},{6,5},{7,4},{8,11},{9,10},{10,... | collective-permute-start | bytes 688136 | tf_op jit(solution)/shard_map/ppermute | solution.py:234
  3.8 11.9 %collective-permute-start.2 = (bf16[1,64,1792]{2,1,0:T(8,128)(2,1)}, bf16[1,64,1792]{2,1,0:T(8,128)(2,1)S(1)}, u32[]{:S(2)}, u32[]{:S(2)}) collective-permute-start(bf16[1,64,1792]{2,1,0:T(8,128)(2,1)} %param.6), channel_id=1, source_target_pairs={{0,4},{1,5},{2,6},{3,7},{4,0},{5,1},{6,2},{7,3},{8,12},{9,13},{10,... | collective-permute-start | bytes 688136 | tf_op jit(solution)/shard_map/ppermute | solution.py:234
  5.8 10.0 %collective-permute-start.3 = (bf16[1,32,1024]{2,1,0:T(8,128)(2,1)}, bf16[1,32,1024]{2,1,0:T(8,128)(2,1)S(1)}, u32[]{:S(2)}, u32[]{:S(2)}) collective-permute-start(bf16[1,32,1024]{2,1,0:T(8,128)(2,1)} %param.7), channel_id=1, source_target_pairs={{0,16},{8,24},{16,0},{24,8},{32,48},{40,56},{48,32},{56,40},{64,80... | collective-permute-start | bytes 196616 | tf_op jit(solution)/shard_map/ppermute | solution.py:234
  15.7 6.9 %collective-permute-start.8 = (bf16[2,32,1024]{2,1,0:T(8,128)(2,1)S(1)}, bf16[2,32,1024]{2,1,0:T(8,128)(2,1)S(1)}, u32[]{:S(2)}, u32[]{:S(2)}) collective-permute-start(bf16[2,32,1024]{2,1,0:T(8,128)(2,1)S(1)} %get-tuple-element.37), channel_id=1, source_target_pairs={{0,32},{8,40},{16,48},{24,56},{32,0},{40,8},{48,16},{56,24},{64,96... | collective-permute-start | bytes 393224 | tf_op jit(solution)/shard_map/ppermute | solution.py:234
  17.3 7.0 %collective-permute-start.9 = (bf16[2,32,1024]{2,1,0:T(8,128)(2,1)S(1)}, bf16[2,32,1024]{2,1,0:T(8,128)(2,1)S(1)}, u32[]{:S(2)}, u32[]{:S(2)}) collective-permute-start(bf16[2,32,1024]{2,1,0:T(8,128)(2,1)S(1)} %get-tuple-element.37), channel_id=1, source_target_pairs={{0,96},{8,104},{16,112},{24,120},{32,64},{40,72},{48,80},{56,88},{... | collective-permute-start | bytes 393224 | tf_op jit(solution)/shard_map/ppermute | solution.py:234
  19.4 10.2 %collective-permute-start.6 = (bf16[1,64,1792]{2,1,0:T(8,128)(2,1)}, bf16[1,64,1792]{2,1,0:T(8,128)(2,1)S(1)}, u32[]{:S(2)}, u32[]{:S(2)}) collective-permute-start(bf16[1,64,1792]{2,1,0:T(8,128)(2,1)} %param.6), channel_id=1, source_target_pairs={{0,6},{1,7},{2,4},{3,5},{4,2},{5,3},{6,0},{7,1},{8,14},{9,15},{10,... | collective-permute-start | bytes 688136 | tf_op jit(solution)/shard_map/ppermute | solution.py:234
  19.7 6.5 %collective-permute-start.10 = (bf16[2,32,1024]{2,1,0:T(8,128)(2,1)S(1)}, bf16[2,32,1024]{2,1,0:T(8,128)(2,1)S(1)}, u32[]{:S(2)}, u32[]{:S(2)}) collective-permute-start(bf16[2,32,1024]{2,1,0:T(8,128)(2,1)S(1)} %get-tuple-element.37), channel_id=1, source_target_pairs={{0,64},{8,72},{16,80},{24,88},{32,96},{40,104},{48,112},{56,120},{... | collective-permute-start | bytes 393224 | tf_op jit(solution)/shard_map/ppermute | solution.py:234
  20.3 10.0 %collective-permute-start.4 = (bf16[1,64,1792]{2,1,0:T(8,128)(2,1)S(1)}, bf16[1,64,1792]{2,1,0:T(8,128)(2,1)S(1)}, u32[]{:S(2)}, u32[]{:S(2)}) collective-permute-start(bf16[1,64,1792]{2,1,0:T(8,128)(2,1)S(1)} %collective-permute-done.rest_0_), channel_id=1, source_target_pairs={{0,3},{1,2},{2,1},{3,0},{4,7},{5,6},{6,5},{7,4},{8,11},{9,10},{10,... | collective-permute-start | bytes 688136 | tf_op jit(solution)/shard_map/ppermute | solution.py:234
  22.6 7.6 %collective-permute-start.5 = (bf16[1,64,1792]{2,1,0:T(8,128)(2,1)S(1)}, bf16[1,64,1792]{2,1,0:T(8,128)(2,1)S(1)}, u32[]{:S(2)}, u32[]{:S(2)}) collective-permute-start(bf16[1,64,1792]{2,1,0:T(8,128)(2,1)S(1)} %collective-permute-done.2.rest_3_), channel_id=1, source_target_pairs={{0,1},{1,0},{2,3},{3,2},{4,5},{5,4},{6,7},{7,6},{8,9},{9,8},{10,11... | collective-permute-start | bytes 688136 | tf_op jit(solution)/shard_map/ppermute | solution.py:234
  24.3 7.6 %collective-permute-start.7 = (bf16[1,64,1792]{2,1,0:T(8,128)(2,1)S(1)}, bf16[1,64,1792]{2,1,0:T(8,128)(2,1)S(1)}, u32[]{:S(2)}, u32[]{:S(2)}) collective-permute-start(bf16[1,64,1792]{2,1,0:T(8,128)(2,1)S(1)} %collective-permute-done.1.rest_2_), channel_id=1, source_target_pairs={{0,4},{1,5},{2,6},{3,7},{4,0},{5,1},{6,2},{7,3},{8,12},{9,13},{10,... | collective-permute-start | bytes 688136 | tf_op jit(solution)/shard_map/ppermute | solution.py:234
  31.9 1.9 %collective-permute-start.11 = (bf16[8,32,1024]{2,1,0:T(8,128)(2,1)S(1)}, bf16[8,32,1024]{2,1,0:T(8,128)(2,1)S(1)}, u32[]{:S(2)}, u32[]{:S(2)}) collective-permute-start(bf16[8,32,1024]{2,1,0:T(8,128)(2,1)S(1)} %constant_dynamic-update-slice_fusion.2.rest_8_), channel_id=1, source_target_pairs={{0,8},{8,0},{16,24},{24,16},{32,40},{40,32},{48,56},{56,48},{64,72... | collective-permute-start | bytes 1572872 | tf_op jit(solution)/shard_map/ppermute | solution.py:234

commit v6 on v5

--- a/solution.py
+++ b/solution.py
@@ -21,6 +21,7 @@
 CHUNK = 64
 PLACE_SLOTS = 2
 PLACE_ROWS = 32
+EARLY_BLOCKS = 2
 
 
 def parity(values):
@@ -57,9 +58,14 @@
     return xs
 
 
+def scale_factor(v, flips):
+    return flips.astype(jnp.float32) / (v * lax.rsqrt(v) + EPSILON)
+
+
 def local_kernel(
     acts_masks, grads_masks, moment_ref, flips_ref, place_ref, lane_ref, sign_ref, *rest
 ):
+    early_factors, rest = rest[:EARLY_BLOCKS], rest[EARLY_BLOCKS:]
     acts_pieces, rest = rest[: len(acts_masks)], rest[len(acts_masks) :]
     grads_pieces, rest = rest[: len(grads_masks)], rest[len(grads_masks) :]
     out_ref, acts_ref, grads_ref, moment, flips, scaled, half, inner, whole, *rest = rest
@@ -87,7 +93,7 @@
             place_sem.at[slot],
         )
 
-    for block in range(blocks):
+    for block in range(EARLY_BLOCKS, blocks):
         for copy in block_copies(block):
             copy.start()
     for slot in range(len(places)):
@@ -111,8 +117,10 @@
         acts = acts_ref[:, rows]
         for strip in range(strips):
             cols = slice(strip * TILE, (strip + 1) * TILE)
-            v = moment[rows, cols]
-            factor = flips[rows, cols].astype(jnp.float32) / (v * lax.rsqrt(v) + EPSILON)
+            if isinstance(block, int) and block < EARLY_BLOCKS:
+                factor = early_factors[block][:, cols]
+            else:
+                factor = scale_factor(moment[rows, cols], flips[rows, cols])
             scaled[:, cols] = dot(acts, grads_ref[:, cols], 0) * factor
 
     def transform_cols():
@@ -141,9 +149,7 @@
         for copy in block_copies(block):
             copy.wait()
 
-    wait_for(0)
     scale(0)
-    wait_for(1)
     transform_cols()
     scale(1)
 
@@ -200,7 +206,7 @@
                 place_copy(group + len(places), slot).start()
 
 
-def local_contributions(acts, grads, moment, flips, place, lane, sign):
+def local_contributions(acts, grads, moment, flips, early_factors, place, lane, sign):
     hidden, width = moment.shape
     acts_masks, acts = zip(*acts)
     grads_masks, grads = zip(*grads)
@@ -210,7 +216,7 @@
     return pl.pallas_call(
         functools.partial(local_kernel, acts_masks, grads_masks),
         out_shape=jax.ShapeDtypeStruct(place.shape, jnp.float32),
-        in_specs=[in_hbm] * 2 + [in_vmem] * (3 + len(acts) + len(grads)),
+        in_specs=[in_hbm] * 2 + [in_vmem] * (3 + EARLY_BLOCKS + len(acts) + len(grads)),
         out_specs=in_vmem,
         scratch_shapes=[
             pltpu.VMEM((tokens, hidden), jnp.bfloat16),
@@ -227,14 +233,14 @@
             pltpu.SemaphoreType.DMA((PLACE_SLOTS,)),
         ],
         compiler_params=pltpu.CompilerParams(vmem_limit_bytes=48 * 2**20),
-    )(moment, flips, place, lane, sign, *acts, *grads)
+    )(moment, flips, place, lane, sign, *early_factors, *acts, *grads)
 
 
 def swap(x, axis, mask):
     return lax.ppermute(x, axis, [(i, i ^ mask) for i in range(lax.axis_size(axis))])
 
 
-def gather(acts, grads, meanwhile):
+def gather(acts, grads, meanwhile, later):
     own = grads[None]
     near = swap(own, "row", 2)
     held = {0: acts[None]}
@@ -249,11 +255,11 @@
     held[6] = far
     pair = jnp.concatenate([own, near])
     half = jnp.concatenate([pair] + [swap(pair, "row", mask) for mask in (4, 12, 8)])
-    held, half = lax.optimization_barrier((held, half))
+    held, half, later = lax.optimization_barrier((held, half, later))
     other = swap(half, "row", 1)
     acts = [((mask,), piece) for mask, piece in held.items() if mask] + [((0,), mine)]
     masks = tuple(far ^ near for far in (0, 4, 12, 8) for near in (0, 2))
-    return acts, [(masks, half), (tuple(mask ^ 1 for mask in masks), other)], meanwhile
+    return acts, [(masks, half), (tuple(mask ^ 1 for mask in masks), other)], meanwhile, later
 
 
 def shards(hidden_acts, out_grads, second_moment, sign_flips, kept_rows, kept_cols):
@@ -270,8 +276,16 @@
         lane = cols % LANES
         flips = parity(rows // GROUP_PAD & my_row) ^ parity(cols // width & my_col)
         sign = jnp.where(flips == 1, -NORM_SCALE, NORM_SCALE)
-        acts, grads, picks = gather(hidden_acts[example], out_grads[example], (place, lane, sign))
-        contribution = local_contributions(acts, grads, second_moment, sign_flips, *picks)
+        early = [
+            scale_factor(second_moment[start : start + TILE], sign_flips[start : start + TILE])
+            for start in range(0, EARLY_BLOCKS * TILE, TILE)
+        ]
+        acts, grads, (first, *picks), later = gather(
+            hidden_acts[example], out_grads[example], (early[0], place, lane, sign), early[1:]
+        )
+        contribution = local_contributions(
+            acts, grads, second_moment, sign_flips, [first, *later], *picks
+        )
         received = lax.all_to_all(contribution, ("row", "col"), 0, 0, tiled=True)
         outs.append(jnp.sum(received, axis=0))
     return jnp.stack(outs)

time: 69.6 us -> 68.5 us (0.984)
  waiting for transfers between devices: 12.8 us -> 6.68 us
  starting transfers between devices: 17.2 us -> 20.9 us
  other arithmetic: 2.65 us -> 5.05 us
  Pallas kernels: 19.6 us -> 18.7 us
    ppermute x12, waiting for transfers between devices: 12.8 us -> 6.68 us  [swap(): lax.ppermute(x, axis, [(i, i ^ mask) for i in range(lax.axis_size(axis))])]
    ppermute x12, starting transfers between devices: 17.2 us -> 20.9 us  [swap(): lax.ppermute(x, axis, [(i, i ^ mask) for i in range(lax.axis_size(axis))])]
    div x0 -> x1, other arithmetic: none -> 2.4 us  [scale_factor(): return flips.astype(jnp.float32) / (v * lax.rsqrt(v) + EPSILON)]
    pallas_call x1, Pallas kernels: 19.6 us -> 18.7 us  [local_contributions(): pl.pallas_call(functools.partial(local_kernel, acts_masks, grads_masks),...]
  transfers between devices with their start and end apart: 12 -> 12, of which waited for: 7 -> 4; matrix products, arithmetic and copies ran while one was open for 6% -> 9% of each run, Pallas kernels for 0% -> 0%
where the time goes in v6:
time: 68.5 us; the launch traced here: 67.5 us
  starting transfers between devices  20.9 us (31%)
  Pallas kernels  18.7 us (27%)
  blocking collectives  14.2 us (21%)
  waiting for transfers between devices  6.68 us (10%)
  other arithmetic  5.05 us (7%)
  local copies, waits for them, and re-layouts  1.86 us (3%)
    ppermute x12, starting transfers between devices, swap(): lax.ppermute(x, axis, [(i, i ^ mask) for i in range(lax.axis_size(axis))])  20.9 us
    pallas_call x1, Pallas kernels, local_contributions(): pl.pallas_call(functools.partial(local_kernel, acts_masks, grads_masks),...  18.7 us
    all_to_all x1, blocking collectives, shards(): received = lax.all_to_all(contribution, ('row', 'col'), 0, 0, tiled=True)  14.2 us
    ppermute x12, waiting for transfers between devices, swap(): lax.ppermute(x, axis, [(i, i ^ mask) for i in range(lax.axis_size(axis))])  6.68 us
    div x1, other arithmetic, scale_factor(): return flips.astype(jnp.float32) / (v * lax.rsqrt(v) + EPSILON)  2.4 us
  transfers between devices with their start and end apart: 12, of which 4 were waited for; matrix products, arithmetic and copies ran while one was open for 9% of the time, Pallas kernels for 0%

profile of v6, /device:TPU:0, one launch (start us, length us, event | category | flops | bytes accessed | tf_op | source)
XLA Modules:
  0.0 67.5 jit_solution(7637137050727826474)
XLA Ops:
  0.0 2.0 %collective-permute-start.2 = (bf16[1,64,1792]{2,1,0:T(8,128)(2,1)}, bf16[1,64,1792]{2,1,0:T(8,128)(2,1)S(1)}, u32[]{:S(2)}, u32[]{:S(2)}) collective-permute-start(bf16[1,64,1792]{2,1,0:T(8,128)(2,1)} %param.6), channel_id=1, source_target_pairs={{0,4},{1,5},{2,6},{3,7},{4,0},{5,1},{6,2},{7,3},{8,12},{9,13},{10,... | collective-permute-start | bytes 688136 | tf_op jit(solution)/shard_map/ppermute | solution.py:240
  2.0 3.0 %collective-permute-start.1 = (bf16[1,64,1792]{2,1,0:T(8,128)(2,1)}, bf16[1,64,1792]{2,1,0:T(8,128)(2,1)S(1)}, u32[]{:S(2)}, u32[]{:S(2)}) collective-permute-start(bf16[1,64,1792]{2,1,0:T(8,128)(2,1)} %param.6), channel_id=1, source_target_pairs={{0,3},{1,2},{2,1},{3,0},{4,7},{5,6},{6,5},{7,4},{8,11},{9,10},{10,... | collective-permute-start | bytes 688136 | tf_op jit(solution)/shard_map/ppermute | solution.py:240
  5.0 0.1 collective-permute-start
  5.2 3.6 %collective-permute-start.3 = (bf16[1,32,1024]{2,1,0:T(8,128)(2,1)}, bf16[1,32,1024]{2,1,0:T(8,128)(2,1)S(1)}, u32[]{:S(2)}, u32[]{:S(2)}) collective-permute-start(bf16[1,32,1024]{2,1,0:T(8,128)(2,1)} %param.7), channel_id=1, source_target_pairs={{0,16},{8,24},{16,0},{24,8},{32,48},{40,56},{48,32},{56,40},{64,80... | collective-permute-start | bytes 196616 | tf_op jit(solution)/shard_map/ppermute | solution.py:240
  8.7 1.0 %add_select_fusion.2 = (s32[128,128]{1,0:T(8,128)S(1)}, s32[128,128]{1,0:T(8,128)S(1)}) fusion(s32[128,128]{1,0:T(8,128)} %bitcast.7, s32[128,128]{1,0:T(8,128)} %bitcast.9), kind=kLoop, calls=%fused_computation.18 | loop fusion | flops 770048 | bytes 262144 | tf_op jit(solution)/shard_map/jit(remainder)/select_n | solution.py:276
  9.7 2.4 %fusion.3 = (f32[256,1024]{1,0:T(8,128)S(1)}, f32[256,1024]{1,0:T(8,128)S(1)}) fusion(f32[1792,1024]{1,0:T(8,128)} %moment_ref.1, bf16[1792,1024]{1,0:T(8,128)(2,1)} %flips_ref.1), kind=kLoop, calls=%fused_computation.5 | loop fusion | flops 2097152 | bytes 5242880 | tf_op jit(solution)/shard_map/div | solution.py:62
  12.1 1.0 %compare_select_fusion.sign_ref = f32[128,128]{1,0:T(8,128)S(1)} fusion(s32[128,128]{1,0:T(8,128)} %bitcast.8, s32[128,128]{1,0:T(8,128)} %bitcast.10, s32[]{:T(128)S(6)} %axis_index.25, s32[]{:T(128)S(6)} %axis_index.23), kind=kLoop, calls=%fused_computation.44 | loop fusion | flops 868352 | bytes 196616 | tf_op jit(solution)/shard_map/jit(_where)/select_n | solution.py:278
  13.1 1.0 %pad.4.rest_9_ = bf16[2,64,1792]{2,1,0:T(8,128)(2,1)S(1)} pad(bf16[1,64,1792]{2,1,0:T(8,128)(2,1)} %param.6, bf16[]{:T(256)} %constant.73.clone.1), padding=0_1x0_0x0_0 | pad | bytes 688130 | tf_op jit(solution)/shard_map/jit(_pad)/pad | solution.py:250
  14.1 0.9 %constant_dynamic-update-slice_fusion.1 = (bf16[2,32,1024]{2,1,0:T(8,128)(2,1)S(1)}, bf16[8,32,1024]{2,1,0:T(8,128)(2,1)S(1)}) fusion(bf16[1,32,1024]{2,1,0:T(8,128)(2,1)} %param.7), kind=kLoop, calls=%fused_computation.48 | loop fusion | bytes 196608
  15.0 0.0 collective-permute-done.3
  15.0 0.0 collective-permute-done.2.rest_5_
  15.0 0.0 collective-permute-done.1.rest_4_
  15.0 0.0 collective-permute-done.rest_2_
  15.0 1.6 %collective-permute-start.8 = (bf16[2,32,1024]{2,1,0:T(8,128)(2,1)S(1)}, bf16[2,32,1024]{2,1,0:T(8,128)(2,1)S(1)}, u32[]{:S(2)}, u32[]{:S(2)}) collective-permute-start(bf16[2,32,1024]{2,1,0:T(8,128)(2,1)S(1)} %get-tuple-element.43), channel_id=1, source_target_pairs={{0,32},{8,40},{16,48},{24,56},{32,0},{40,8},{48,16},{56,24},{64,96... | collective-permute-start | bytes 393224 | tf_op jit(solution)/shard_map/ppermute | solution.py:240
  16.6 2.1 %collective-permute-start.9 = (bf16[2,32,1024]{2,1,0:T(8,128)(2,1)S(1)}, bf16[2,32,1024]{2,1,0:T(8,128)(2,1)S(1)}, u32[]{:S(2)}, u32[]{:S(2)}) collective-permute-start(bf16[2,32,1024]{2,1,0:T(8,128)(2,1)S(1)} %get-tuple-element.43), channel_id=1, source_target_pairs={{0,96},{8,104},{16,112},{24,120},{32,64},{40,72},{48,80},{56,88},{... | collective-permute-start | bytes 393224 | tf_op jit(solution)/shard_map/ppermute | solution.py:240
  18.7 0.8 %collective-permute-start.6 = (bf16[1,64,1792]{2,1,0:T(8,128)(2,1)}, bf16[1,64,1792]{2,1,0:T(8,128)(2,1)S(1)}, u32[]{:S(2)}, u32[]{:S(2)}) collective-permute-start(bf16[1,64,1792]{2,1,0:T(8,128)(2,1)} %param.6), channel_id=1, source_target_pairs={{0,6},{1,7},{2,4},{3,5},{4,2},{5,3},{6,0},{7,1},{8,14},{9,15},{10,... | collective-permute-start | bytes 688136 | tf_op jit(solution)/shard_map/ppermute | solution.py:240
  19.5 0.6 collective-permute-start.10
  20.1 3.0 %collective-permute-start.4 = (bf16[1,64,1792]{2,1,0:T(8,128)(2,1)S(1)}, bf16[1,64,1792]{2,1,0:T(8,128)(2,1)S(1)}, u32[]{:S(2)}, u32[]{:S(2)}) collective-permute-start(bf16[1,64,1792]{2,1,0:T(8,128)(2,1)S(1)} %collective-permute-done.rest_2_), channel_id=1, source_target_pairs={{0,3},{1,2},{2,1},{3,0},{4,7},{5,6},{6,5},{7,4},{8,11},{9,10},{10,... | collective-permute-start | bytes 688136 | tf_op jit(solution)/shard_map/ppermute | solution.py:240
  23.1 0.0 collective-permute-done.8
  23.1 2.2 %collective-permute-start.7 = (bf16[1,64,1792]{2,1,0:T(8,128)(2,1)S(1)}, bf16[1,64,1792]{2,1,0:T(8,128)(2,1)S(1)}, u32[]{:S(2)}, u32[]{:S(2)}) collective-permute-start(bf16[1,64,1792]{2,1,0:T(8,128)(2,1)S(1)} %collective-permute-done.1.rest_4_), channel_id=1, source_target_pairs={{0,4},{1,5},{2,6},{3,7},{4,0},{5,1},{6,2},{7,3},{8,12},{9,13},{10,... | collective-permute-start | bytes 688136 | tf_op jit(solution)/shard_map/ppermute | solution.py:240
  25.4 0.0 collective-permute-done.9
  25.4 1.9 %collective-permute-start.5 = (bf16[1,64,1792]{2,1,0:T(8,128)(2,1)S(1)}, bf16[1,64,1792]{2,1,0:T(8,128)(2,1)S(1)}, u32[]{:S(2)}, u32[]{:S(2)}) collective-permute-start(bf16[1,64,1792]{2,1,0:T(8,128)(2,1)S(1)} %collective-permute-done.2.rest_5_), channel_id=1, source_target_pairs={{0,1},{1,0},{2,3},{3,2},{4,5},{5,4},{6,7},{7,6},{8,9},{9,8},{10,11... | collective-permute-start | bytes 688136 | tf_op jit(solution)/shard_map/ppermute | solution.py:240
  27.3 0.0 collective-permute-done.10
  27.3 2.4 %collective-permute-done.6.rest_7_ = bf16[1,64,1792]{2,1,0:T(8,128)(2,1)S(1)} collective-permute-done((bf16[1,64,1792]{2,1,0:T(8,128)(2,1)}, bf16[1,64,1792]{2,1,0:T(8,128)(2,1)S(1)}, u32[]{:S(2)}, u32[]{:S(2)}) %collective-permute-start.6) | collective-permute-done | bytes 229408 | tf_op jit(solution)/shard_map/ppermute | solution.py:240
  29.7 0.6 collective-permute-done.4.rest_3_
  30.4 1.7 %collective-permute-done.7.rest_8_ = bf16[1,64,1792]{2,1,0:T(8,128)(2,1)S(1)} collective-permute-done((bf16[1,64,1792]{2,1,0:T(8,128)(2,1)S(1)}, bf16[1,64,1792]{2,1,0:T(8,128)(2,1)S(1)}, u32[]{:S(2)}, u32[]{:S(2)}) %collective-permute-start.7) | collective-permute-done | bytes 229408 | tf_op jit(solution)/shard_map/ppermute | solution.py:240
  32.1 0.0 collective-permute-done.5.rest_6_
  32.1 0.0 collective-permute-start.11
  32.1 1.9 %collective-permute-done.11.rest_11_ = bf16[8,32,1024]{2,1,0:T(8,128)(2,1)S(1)} collective-permute-done((bf16[8,32,1024]{2,1,0:T(8,128)(2,1)S(1)}, bf16[8,32,1024]{2,1,0:T(8,128)(2,1)S(1)}, u32[]{:S(2)}, u32[]{:S(2)}) %collective-permute-start.11) | collective-permute-done | bytes 524320 | tf_op jit(solution)/shard_map/ppermute | solution.py:240
  34.0 18.7 %shard_map.64 = f32[128,128]{1,0:T(8,128)S(1)} custom-call(f32[1792,1024]{1,0:T(8,128)} %moment_ref.1, bf16[1792,1024]{1,0:T(8,128)(2,1)} %flips_ref.1, s32[128,128]{1,0:T(8,128)S(1)} %get-tuple-element.23.place_ref, s32[128,128]{1,0:T(8,128)S(1)} %get-tuple-element.24.lane_ref, f32[128,128]{1,0:T(8,128)S(1)} %compare_select_fusion.sign_ref, ...), custom_call_target="tpu_custom_call" | custom-call | tf_op jit(solution)/shard_map/pallas_call | solution.py:216
  52.6 14.2 %all_to_all.9 = f32[128,1,128]{2,1,0:T(1,128)S(1)} all-to-all(f32[128,1,128]{2,1,0:T(1,128)S(1)} %bitcast.6), channel_id=1, replica_groups=mesh['row'=16,'col'=8] {'row','col'}, dimensions={0} | all-to-all | bytes 131072 | tf_op jit(solution)/shard_map/all_to_all | solution.py:289
  66.8 0.7 reduce_sum.9
  (4 shorter events, 0.0 us)
Async XLA Ops:
  0.0 15.0 %collective-permute-start.2 = (bf16[1,64,1792]{2,1,0:T(8,128)(2,1)}, bf16[1,64,1792]{2,1,0:T(8,128)(2,1)S(1)}, u32[]{:S(2)}, u32[]{:S(2)}) collective-permute-start(bf16[1,64,1792]{2,1,0:T(8,128)(2,1)} %param.6), channel_id=1, source_target_pairs={{0,4},{1,5},{2,6},{3,7},{4,0},{5,1},{6,2},{7,3},{8,12},{9,13},{10,... | collective-permute-start | bytes 688136 | tf_op jit(solution)/shard_map/ppermute | solution.py:240
  2.0 13.0 %collective-permute-start.1 = (bf16[1,64,1792]{2,1,0:T(8,128)(2,1)}, bf16[1,64,1792]{2,1,0:T(8,128)(2,1)S(1)}, u32[]{:S(2)}, u32[]{:S(2)}) collective-permute-start(bf16[1,64,1792]{2,1,0:T(8,128)(2,1)} %param.6), channel_id=1, source_target_pairs={{0,3},{1,2},{2,1},{3,0},{4,7},{5,6},{6,5},{7,4},{8,11},{9,10},{10,... | collective-permute-start | bytes 688136 | tf_op jit(solution)/shard_map/ppermute | solution.py:240
  5.0 10.0 %collective-permute-start = (bf16[1,64,1792]{2,1,0:T(8,128)(2,1)}, bf16[1,64,1792]{2,1,0:T(8,128)(2,1)S(1)}, u32[]{:S(2)}, u32[]{:S(2)}) collective-permute-start(bf16[1,64,1792]{2,1,0:T(8,128)(2,1)} %param.6), channel_id=1, source_target_pairs={{0,1},{1,0},{2,3},{3,2},{4,5},{5,4},{6,7},{7,6},{8,9},{9,8},{10,11... | collective-permute-start | bytes 688136 | tf_op jit(solution)/shard_map/ppermute | solution.py:240
  5.2 9.8 %collective-permute-start.3 = (bf16[1,32,1024]{2,1,0:T(8,128)(2,1)}, bf16[1,32,1024]{2,1,0:T(8,128)(2,1)S(1)}, u32[]{:S(2)}, u32[]{:S(2)}) collective-permute-start(bf16[1,32,1024]{2,1,0:T(8,128)(2,1)} %param.7), channel_id=1, source_target_pairs={{0,16},{8,24},{16,0},{24,8},{32,48},{40,56},{48,32},{56,40},{64,80... | collective-permute-start | bytes 196616 | tf_op jit(solution)/shard_map/ppermute | solution.py:240
  15.0 8.1 %collective-permute-start.8 = (bf16[2,32,1024]{2,1,0:T(8,128)(2,1)S(1)}, bf16[2,32,1024]{2,1,0:T(8,128)(2,1)S(1)}, u32[]{:S(2)}, u32[]{:S(2)}) collective-permute-start(bf16[2,32,1024]{2,1,0:T(8,128)(2,1)S(1)} %get-tuple-element.43), channel_id=1, source_target_pairs={{0,32},{8,40},{16,48},{24,56},{32,0},{40,8},{48,16},{56,24},{64,96... | collective-permute-start | bytes 393224 | tf_op jit(solution)/shard_map/ppermute | solution.py:240
  16.6 8.8 %collective-permute-start.9 = (bf16[2,32,1024]{2,1,0:T(8,128)(2,1)S(1)}, bf16[2,32,1024]{2,1,0:T(8,128)(2,1)S(1)}, u32[]{:S(2)}, u32[]{:S(2)}) collective-permute-start(bf16[2,32,1024]{2,1,0:T(8,128)(2,1)S(1)} %get-tuple-element.43), channel_id=1, source_target_pairs={{0,96},{8,104},{16,112},{24,120},{32,64},{40,72},{48,80},{56,88},{... | collective-permute-start | bytes 393224 | tf_op jit(solution)/shard_map/ppermute | solution.py:240
  18.7 11.0 %collective-permute-start.6 = (bf16[1,64,1792]{2,1,0:T(8,128)(2,1)}, bf16[1,64,1792]{2,1,0:T(8,128)(2,1)S(1)}, u32[]{:S(2)}, u32[]{:S(2)}) collective-permute-start(bf16[1,64,1792]{2,1,0:T(8,128)(2,1)} %param.6), channel_id=1, source_target_pairs={{0,6},{1,7},{2,4},{3,5},{4,2},{5,3},{6,0},{7,1},{8,14},{9,15},{10,... | collective-permute-start | bytes 688136 | tf_op jit(solution)/shard_map/ppermute | solution.py:240
  19.5 7.8 %collective-permute-start.10 = (bf16[2,32,1024]{2,1,0:T(8,128)(2,1)S(1)}, bf16[2,32,1024]{2,1,0:T(8,128)(2,1)S(1)}, u32[]{:S(2)}, u32[]{:S(2)}) collective-permute-start(bf16[2,32,1024]{2,1,0:T(8,128)(2,1)S(1)} %get-tuple-element.43), channel_id=1, source_target_pairs={{0,64},{8,72},{16,80},{24,88},{32,96},{40,104},{48,112},{56,120},{... | collective-permute-start | bytes 393224 | tf_op jit(solution)/shard_map/ppermute | solution.py:240
  20.1 10.3 %collective-permute-start.4 = (bf16[1,64,1792]{2,1,0:T(8,128)(2,1)S(1)}, bf16[1,64,1792]{2,1,0:T(8,128)(2,1)S(1)}, u32[]{:S(2)}, u32[]{:S(2)}) collective-permute-start(bf16[1,64,1792]{2,1,0:T(8,128)(2,1)S(1)} %collective-permute-done.rest_2_), channel_id=1, source_target_pairs={{0,3},{1,2},{2,1},{3,0},{4,7},{5,6},{6,5},{7,4},{8,11},{9,10},{10,... | collective-permute-start | bytes 688136 | tf_op jit(solution)/shard_map/ppermute | solution.py:240
  23.1 8.9 %collective-permute-start.7 = (bf16[1,64,1792]{2,1,0:T(8,128)(2,1)S(1)}, bf16[1,64,1792]{2,1,0:T(8,128)(2,1)S(1)}, u32[]{:S(2)}, u32[]{:S(2)}) collective-permute-start(bf16[1,64,1792]{2,1,0:T(8,128)(2,1)S(1)} %collective-permute-done.1.rest_4_), channel_id=1, source_target_pairs={{0,4},{1,5},{2,6},{3,7},{4,0},{5,1},{6,2},{7,3},{8,12},{9,13},{10,... | collective-permute-start | bytes 688136 | tf_op jit(solution)/shard_map/ppermute | solution.py:240
  25.4 6.7 %collective-permute-start.5 = (bf16[1,64,1792]{2,1,0:T(8,128)(2,1)S(1)}, bf16[1,64,1792]{2,1,0:T(8,128)(2,1)S(1)}, u32[]{:S(2)}, u32[]{:S(2)}) collective-permute-start(bf16[1,64,1792]{2,1,0:T(8,128)(2,1)S(1)} %collective-permute-done.2.rest_5_), channel_id=1, source_target_pairs={{0,1},{1,0},{2,3},{3,2},{4,5},{5,4},{6,7},{7,6},{8,9},{9,8},{10,11... | collective-permute-start | bytes 688136 | tf_op jit(solution)/shard_map/ppermute | solution.py:240
  32.1 1.9 %collective-permute-start.11 = (bf16[8,32,1024]{2,1,0:T(8,128)(2,1)S(1)}, bf16[8,32,1024]{2,1,0:T(8,128)(2,1)S(1)}, u32[]{:S(2)}, u32[]{:S(2)}) collective-permute-start(bf16[8,32,1024]{2,1,0:T(8,128)(2,1)S(1)} %constant_dynamic-update-slice_fusion.2.rest_10_), channel_id=1, source_target_pairs={{0,8},{8,0},{16,24},{24,16},{32,40},{40,32},{48,56},{56,48},{64,72... | collective-permute-start | bytes 1572872 | tf_op jit(solution)/shard_map/ppermute | solution.py:240

commit v7 on v6

--- a/solution.py
+++ b/solution.py
@@ -93,7 +93,7 @@
             place_sem.at[slot],
         )
 
-    for block in range(EARLY_BLOCKS, blocks):
+    for block in range(EARLY_BLOCKS, EARLY_BLOCKS + 2):
         for copy in block_copies(block):
             copy.start()
     for slot in range(len(places)):
@@ -150,6 +150,9 @@
             copy.wait()
 
     scale(0)
+    for block in range(EARLY_BLOCKS + 2, blocks):
+        for copy in block_copies(block):
+            copy.start()
     transform_cols()
     scale(1)
 

time: 68.5 us -> 68.5 us (level)
  no operation moved by 1% of the time
where the time goes in v7:
time: 68.5 us; the launch traced here: 67.5 us
  starting transfers between devices  20.9 us (31%)
  Pallas kernels  18.7 us (27%)
  blocking collectives  14.2 us (21%)
  waiting for transfers between devices  6.68 us (10%)
  other arithmetic  5.05 us (7%)
  local copies, waits for them, and re-layouts  1.86 us (3%)
    ppermute x12, starting transfers between devices, swap(): lax.ppermute(x, axis, [(i, i ^ mask) for i in range(lax.axis_size(axis))])  20.9 us
    pallas_call x1, Pallas kernels, local_contributions(): pl.pallas_call(functools.partial(local_kernel, acts_masks, grads_masks),...  18.7 us
    all_to_all x1, blocking collectives, shards(): received = lax.all_to_all(contribution, ('row', 'col'), 0, 0, tiled=True)  14.2 us
    ppermute x12, waiting for transfers between devices, swap(): lax.ppermute(x, axis, [(i, i ^ mask) for i in range(lax.axis_size(axis))])  6.68 us
    div x1, other arithmetic, scale_factor(): return flips.astype(jnp.float32) / (v * lax.rsqrt(v) + EPSILON)  2.4 us
  transfers between devices with their start and end apart: 12, of which 4 were waited for; matrix products, arithmetic and copies ran while one was open for 9% of the time, Pallas kernels for 0%

profile of v7, /device:TPU:0, one launch (start us, length us, event | category | flops | bytes accessed | tf_op | source)
XLA Modules:
  0.0 67.5 jit_solution(10648114551730053437)
XLA Ops:
  0.0 2.0 %collective-permute-start.2 = (bf16[1,64,1792]{2,1,0:T(8,128)(2,1)}, bf16[1,64,1792]{2,1,0:T(8,128)(2,1)S(1)}, u32[]{:S(2)}, u32[]{:S(2)}) collective-permute-start(bf16[1,64,1792]{2,1,0:T(8,128)(2,1)} %param.6), channel_id=1, source_target_pairs={{0,4},{1,5},{2,6},{3,7},{4,0},{5,1},{6,2},{7,3},{8,12},{9,13},{10,... | collective-permute-start | bytes 688136 | tf_op jit(solution)/shard_map/ppermute | solution.py:243
  2.0 3.0 %collective-permute-start.1 = (bf16[1,64,1792]{2,1,0:T(8,128)(2,1)}, bf16[1,64,1792]{2,1,0:T(8,128)(2,1)S(1)}, u32[]{:S(2)}, u32[]{:S(2)}) collective-permute-start(bf16[1,64,1792]{2,1,0:T(8,128)(2,1)} %param.6), channel_id=1, source_target_pairs={{0,3},{1,2},{2,1},{3,0},{4,7},{5,6},{6,5},{7,4},{8,11},{9,10},{10,... | collective-permute-start | bytes 688136 | tf_op jit(solution)/shard_map/ppermute | solution.py:243
  5.0 0.1 collective-permute-start
  5.2 3.6 %collective-permute-start.3 = (bf16[1,32,1024]{2,1,0:T(8,128)(2,1)}, bf16[1,32,1024]{2,1,0:T(8,128)(2,1)S(1)}, u32[]{:S(2)}, u32[]{:S(2)}) collective-permute-start(bf16[1,32,1024]{2,1,0:T(8,128)(2,1)} %param.7), channel_id=1, source_target_pairs={{0,16},{8,24},{16,0},{24,8},{32,48},{40,56},{48,32},{56,40},{64,80... | collective-permute-start | bytes 196616 | tf_op jit(solution)/shard_map/ppermute | solution.py:243
  8.7 1.0 %add_select_fusion.2 = (s32[128,128]{1,0:T(8,128)S(1)}, s32[128,128]{1,0:T(8,128)S(1)}) fusion(s32[128,128]{1,0:T(8,128)} %bitcast.7, s32[128,128]{1,0:T(8,128)} %bitcast.9), kind=kLoop, calls=%fused_computation.18 | loop fusion | flops 770048 | bytes 262144 | tf_op jit(solution)/shard_map/jit(remainder)/select_n | solution.py:279
  9.7 2.4 %fusion.3 = (f32[256,1024]{1,0:T(8,128)S(1)}, f32[256,1024]{1,0:T(8,128)S(1)}) fusion(f32[1792,1024]{1,0:T(8,128)} %moment_ref.1, bf16[1792,1024]{1,0:T(8,128)(2,1)} %flips_ref.1), kind=kLoop, calls=%fused_computation.5 | loop fusion | flops 2097152 | bytes 5242880 | tf_op jit(solution)/shard_map/div | solution.py:62
  12.1 1.0 %compare_select_fusion.sign_ref = f32[128,128]{1,0:T(8,128)S(1)} fusion(s32[128,128]{1,0:T(8,128)} %bitcast.8, s32[128,128]{1,0:T(8,128)} %bitcast.10, s32[]{:T(128)S(6)} %axis_index.25, s32[]{:T(128)S(6)} %axis_index.23), kind=kLoop, calls=%fused_computation.44 | loop fusion | flops 868352 | bytes 196616 | tf_op jit(solution)/shard_map/jit(_where)/select_n | solution.py:281
  13.1 1.0 %pad.4.rest_9_ = bf16[2,64,1792]{2,1,0:T(8,128)(2,1)S(1)} pad(bf16[1,64,1792]{2,1,0:T(8,128)(2,1)} %param.6, bf16[]{:T(256)} %constant.73.clone.1), padding=0_1x0_0x0_0 | pad | bytes 688130 | tf_op jit(solution)/shard_map/jit(_pad)/pad | solution.py:253
  14.1 0.9 %constant_dynamic-update-slice_fusion.1 = (bf16[2,32,1024]{2,1,0:T(8,128)(2,1)S(1)}, bf16[8,32,1024]{2,1,0:T(8,128)(2,1)S(1)}) fusion(bf16[1,32,1024]{2,1,0:T(8,128)(2,1)} %param.7), kind=kLoop, calls=%fused_computation.48 | loop fusion | bytes 196608
  15.0 0.0 collective-permute-done.3
  15.0 0.0 collective-permute-done.2.rest_5_
  15.0 0.0 collective-permute-done.1.rest_4_
  15.0 0.0 collective-permute-done.rest_2_
  15.0 1.6 %collective-permute-start.8 = (bf16[2,32,1024]{2,1,0:T(8,128)(2,1)S(1)}, bf16[2,32,1024]{2,1,0:T(8,128)(2,1)S(1)}, u32[]{:S(2)}, u32[]{:S(2)}) collective-permute-start(bf16[2,32,1024]{2,1,0:T(8,128)(2,1)S(1)} %get-tuple-element.43), channel_id=1, source_target_pairs={{0,32},{8,40},{16,48},{24,56},{32,0},{40,8},{48,16},{56,24},{64,96... | collective-permute-start | bytes 393224 | tf_op jit(solution)/shard_map/ppermute | solution.py:243
  16.6 2.1 %collective-permute-start.9 = (bf16[2,32,1024]{2,1,0:T(8,128)(2,1)S(1)}, bf16[2,32,1024]{2,1,0:T(8,128)(2,1)S(1)}, u32[]{:S(2)}, u32[]{:S(2)}) collective-permute-start(bf16[2,32,1024]{2,1,0:T(8,128)(2,1)S(1)} %get-tuple-element.43), channel_id=1, source_target_pairs={{0,96},{8,104},{16,112},{24,120},{32,64},{40,72},{48,80},{56,88},{... | collective-permute-start | bytes 393224 | tf_op jit(solution)/shard_map/ppermute | solution.py:243
  18.7 0.8 %collective-permute-start.6 = (bf16[1,64,1792]{2,1,0:T(8,128)(2,1)}, bf16[1,64,1792]{2,1,0:T(8,128)(2,1)S(1)}, u32[]{:S(2)}, u32[]{:S(2)}) collective-permute-start(bf16[1,64,1792]{2,1,0:T(8,128)(2,1)} %param.6), channel_id=1, source_target_pairs={{0,6},{1,7},{2,4},{3,5},{4,2},{5,3},{6,0},{7,1},{8,14},{9,15},{10,... | collective-permute-start | bytes 688136 | tf_op jit(solution)/shard_map/ppermute | solution.py:243
  19.5 0.6 collective-permute-start.10
  20.1 3.0 %collective-permute-start.4 = (bf16[1,64,1792]{2,1,0:T(8,128)(2,1)S(1)}, bf16[1,64,1792]{2,1,0:T(8,128)(2,1)S(1)}, u32[]{:S(2)}, u32[]{:S(2)}) collective-permute-start(bf16[1,64,1792]{2,1,0:T(8,128)(2,1)S(1)} %collective-permute-done.rest_2_), channel_id=1, source_target_pairs={{0,3},{1,2},{2,1},{3,0},{4,7},{5,6},{6,5},{7,4},{8,11},{9,10},{10,... | collective-permute-start | bytes 688136 | tf_op jit(solution)/shard_map/ppermute | solution.py:243
  23.1 0.0 collective-permute-done.8
  23.1 2.2 %collective-permute-start.7 = (bf16[1,64,1792]{2,1,0:T(8,128)(2,1)S(1)}, bf16[1,64,1792]{2,1,0:T(8,128)(2,1)S(1)}, u32[]{:S(2)}, u32[]{:S(2)}) collective-permute-start(bf16[1,64,1792]{2,1,0:T(8,128)(2,1)S(1)} %collective-permute-done.1.rest_4_), channel_id=1, source_target_pairs={{0,4},{1,5},{2,6},{3,7},{4,0},{5,1},{6,2},{7,3},{8,12},{9,13},{10,... | collective-permute-start | bytes 688136 | tf_op jit(solution)/shard_map/ppermute | solution.py:243
  25.4 0.0 collective-permute-done.9
  25.4 1.9 %collective-permute-start.5 = (bf16[1,64,1792]{2,1,0:T(8,128)(2,1)S(1)}, bf16[1,64,1792]{2,1,0:T(8,128)(2,1)S(1)}, u32[]{:S(2)}, u32[]{:S(2)}) collective-permute-start(bf16[1,64,1792]{2,1,0:T(8,128)(2,1)S(1)} %collective-permute-done.2.rest_5_), channel_id=1, source_target_pairs={{0,1},{1,0},{2,3},{3,2},{4,5},{5,4},{6,7},{7,6},{8,9},{9,8},{10,11... | collective-permute-start | bytes 688136 | tf_op jit(solution)/shard_map/ppermute | solution.py:243
  27.3 0.0 collective-permute-done.10
  27.3 2.4 %collective-permute-done.6.rest_7_ = bf16[1,64,1792]{2,1,0:T(8,128)(2,1)S(1)} collective-permute-done((bf16[1,64,1792]{2,1,0:T(8,128)(2,1)}, bf16[1,64,1792]{2,1,0:T(8,128)(2,1)S(1)}, u32[]{:S(2)}, u32[]{:S(2)}) %collective-permute-start.6) | collective-permute-done | bytes 229408 | tf_op jit(solution)/shard_map/ppermute | solution.py:243
  29.7 0.6 collective-permute-done.4.rest_3_
  30.4 1.7 %collective-permute-done.7.rest_8_ = bf16[1,64,1792]{2,1,0:T(8,128)(2,1)S(1)} collective-permute-done((bf16[1,64,1792]{2,1,0:T(8,128)(2,1)S(1)}, bf16[1,64,1792]{2,1,0:T(8,128)(2,1)S(1)}, u32[]{:S(2)}, u32[]{:S(2)}) %collective-permute-start.7) | collective-permute-done | bytes 229408 | tf_op jit(solution)/shard_map/ppermute | solution.py:243
  32.1 0.0 collective-permute-done.5.rest_6_
  32.1 0.0 collective-permute-start.11
  32.1 1.9 %collective-permute-done.11.rest_11_ = bf16[8,32,1024]{2,1,0:T(8,128)(2,1)S(1)} collective-permute-done((bf16[8,32,1024]{2,1,0:T(8,128)(2,1)S(1)}, bf16[8,32,1024]{2,1,0:T(8,128)(2,1)S(1)}, u32[]{:S(2)}, u32[]{:S(2)}) %collective-permute-start.11) | collective-permute-done | bytes 524320 | tf_op jit(solution)/shard_map/ppermute | solution.py:243
  34.0 18.7 %shard_map.64 = f32[128,128]{1,0:T(8,128)S(1)} custom-call(f32[1792,1024]{1,0:T(8,128)} %moment_ref.1, bf16[1792,1024]{1,0:T(8,128)(2,1)} %flips_ref.1, s32[128,128]{1,0:T(8,128)S(1)} %get-tuple-element.23.place_ref, s32[128,128]{1,0:T(8,128)S(1)} %get-tuple-element.24.lane_ref, f32[128,128]{1,0:T(8,128)S(1)} %compare_select_fusion.sign_ref, ...), custom_call_target="tpu_custom_call" | custom-call | tf_op jit(solution)/shard_map/pallas_call | solution.py:219
  52.6 14.2 %all_to_all.9 = f32[128,1,128]{2,1,0:T(1,128)S(1)} all-to-all(f32[128,1,128]{2,1,0:T(1,128)S(1)} %bitcast.6), channel_id=1, replica_groups=mesh['row'=16,'col'=8] {'row','col'}, dimensions={0} | all-to-all | bytes 131072 | tf_op jit(solution)/shard_map/all_to_all | solution.py:292
  66.8 0.7 reduce_sum.9
  (4 shorter events, 0.0 us)
Async XLA Ops:
  0.0 15.0 %collective-permute-start.2 = (bf16[1,64,1792]{2,1,0:T(8,128)(2,1)}, bf16[1,64,1792]{2,1,0:T(8,128)(2,1)S(1)}, u32[]{:S(2)}, u32[]{:S(2)}) collective-permute-start(bf16[1,64,1792]{2,1,0:T(8,128)(2,1)} %param.6), channel_id=1, source_target_pairs={{0,4},{1,5},{2,6},{3,7},{4,0},{5,1},{6,2},{7,3},{8,12},{9,13},{10,... | collective-permute-start | bytes 688136 | tf_op jit(solution)/shard_map/ppermute | solution.py:243
  2.0 13.0 %collective-permute-start.1 = (bf16[1,64,1792]{2,1,0:T(8,128)(2,1)}, bf16[1,64,1792]{2,1,0:T(8,128)(2,1)S(1)}, u32[]{:S(2)}, u32[]{:S(2)}) collective-permute-start(bf16[1,64,1792]{2,1,0:T(8,128)(2,1)} %param.6), channel_id=1, source_target_pairs={{0,3},{1,2},{2,1},{3,0},{4,7},{5,6},{6,5},{7,4},{8,11},{9,10},{10,... | collective-permute-start | bytes 688136 | tf_op jit(solution)/shard_map/ppermute | solution.py:243
  5.0 10.0 %collective-permute-start = (bf16[1,64,1792]{2,1,0:T(8,128)(2,1)}, bf16[1,64,1792]{2,1,0:T(8,128)(2,1)S(1)}, u32[]{:S(2)}, u32[]{:S(2)}) collective-permute-start(bf16[1,64,1792]{2,1,0:T(8,128)(2,1)} %param.6), channel_id=1, source_target_pairs={{0,1},{1,0},{2,3},{3,2},{4,5},{5,4},{6,7},{7,6},{8,9},{9,8},{10,11... | collective-permute-start | bytes 688136 | tf_op jit(solution)/shard_map/ppermute | solution.py:243
  5.2 9.8 %collective-permute-start.3 = (bf16[1,32,1024]{2,1,0:T(8,128)(2,1)}, bf16[1,32,1024]{2,1,0:T(8,128)(2,1)S(1)}, u32[]{:S(2)}, u32[]{:S(2)}) collective-permute-start(bf16[1,32,1024]{2,1,0:T(8,128)(2,1)} %param.7), channel_id=1, source_target_pairs={{0,16},{8,24},{16,0},{24,8},{32,48},{40,56},{48,32},{56,40},{64,80... | collective-permute-start | bytes 196616 | tf_op jit(solution)/shard_map/ppermute | solution.py:243
  15.0 8.1 %collective-permute-start.8 = (bf16[2,32,1024]{2,1,0:T(8,128)(2,1)S(1)}, bf16[2,32,1024]{2,1,0:T(8,128)(2,1)S(1)}, u32[]{:S(2)}, u32[]{:S(2)}) collective-permute-start(bf16[2,32,1024]{2,1,0:T(8,128)(2,1)S(1)} %get-tuple-element.43), channel_id=1, source_target_pairs={{0,32},{8,40},{16,48},{24,56},{32,0},{40,8},{48,16},{56,24},{64,96... | collective-permute-start | bytes 393224 | tf_op jit(solution)/shard_map/ppermute | solution.py:243
  16.6 8.8 %collective-permute-start.9 = (bf16[2,32,1024]{2,1,0:T(8,128)(2,1)S(1)}, bf16[2,32,1024]{2,1,0:T(8,128)(2,1)S(1)}, u32[]{:S(2)}, u32[]{:S(2)}) collective-permute-start(bf16[2,32,1024]{2,1,0:T(8,128)(2,1)S(1)} %get-tuple-element.43), channel_id=1, source_target_pairs={{0,96},{8,104},{16,112},{24,120},{32,64},{40,72},{48,80},{56,88},{... | collective-permute-start | bytes 393224 | tf_op jit(solution)/shard_map/ppermute | solution.py:243
  18.7 11.0 %collective-permute-start.6 = (bf16[1,64,1792]{2,1,0:T(8,128)(2,1)}, bf16[1,64,1792]{2,1,0:T(8,128)(2,1)S(1)}, u32[]{:S(2)}, u32[]{:S(2)}) collective-permute-start(bf16[1,64,1792]{2,1,0:T(8,128)(2,1)} %param.6), channel_id=1, source_target_pairs={{0,6},{1,7},{2,4},{3,5},{4,2},{5,3},{6,0},{7,1},{8,14},{9,15},{10,... | collective-permute-start | bytes 688136 | tf_op jit(solution)/shard_map/ppermute | solution.py:243
  19.5 7.8 %collective-permute-start.10 = (bf16[2,32,1024]{2,1,0:T(8,128)(2,1)S(1)}, bf16[2,32,1024]{2,1,0:T(8,128)(2,1)S(1)}, u32[]{:S(2)}, u32[]{:S(2)}) collective-permute-start(bf16[2,32,1024]{2,1,0:T(8,128)(2,1)S(1)} %get-tuple-element.43), channel_id=1, source_target_pairs={{0,64},{8,72},{16,80},{24,88},{32,96},{40,104},{48,112},{56,120},{... | collective-permute-start | bytes 393224 | tf_op jit(solution)/shard_map/ppermute | solution.py:243
  20.1 10.3 %collective-permute-start.4 = (bf16[1,64,1792]{2,1,0:T(8,128)(2,1)S(1)}, bf16[1,64,1792]{2,1,0:T(8,128)(2,1)S(1)}, u32[]{:S(2)}, u32[]{:S(2)}) collective-permute-start(bf16[1,64,1792]{2,1,0:T(8,128)(2,1)S(1)} %collective-permute-done.rest_2_), channel_id=1, source_target_pairs={{0,3},{1,2},{2,1},{3,0},{4,7},{5,6},{6,5},{7,4},{8,11},{9,10},{10,... | collective-permute-start | bytes 688136 | tf_op jit(solution)/shard_map/ppermute | solution.py:243
  23.1 8.9 %collective-permute-start.7 = (bf16[1,64,1792]{2,1,0:T(8,128)(2,1)S(1)}, bf16[1,64,1792]{2,1,0:T(8,128)(2,1)S(1)}, u32[]{:S(2)}, u32[]{:S(2)}) collective-permute-start(bf16[1,64,1792]{2,1,0:T(8,128)(2,1)S(1)} %collective-permute-done.1.rest_4_), channel_id=1, source_target_pairs={{0,4},{1,5},{2,6},{3,7},{4,0},{5,1},{6,2},{7,3},{8,12},{9,13},{10,... | collective-permute-start | bytes 688136 | tf_op jit(solution)/shard_map/ppermute | solution.py:243
  25.4 6.7 %collective-permute-start.5 = (bf16[1,64,1792]{2,1,0:T(8,128)(2,1)S(1)}, bf16[1,64,1792]{2,1,0:T(8,128)(2,1)S(1)}, u32[]{:S(2)}, u32[]{:S(2)}) collective-permute-start(bf16[1,64,1792]{2,1,0:T(8,128)(2,1)S(1)} %collective-permute-done.2.rest_5_), channel_id=1, source_target_pairs={{0,1},{1,0},{2,3},{3,2},{4,5},{5,4},{6,7},{7,6},{8,9},{9,8},{10,11... | collective-permute-start | bytes 688136 | tf_op jit(solution)/shard_map/ppermute | solution.py:243
  32.1 1.9 %collective-permute-start.11 = (bf16[8,32,1024]{2,1,0:T(8,128)(2,1)S(1)}, bf16[8,32,1024]{2,1,0:T(8,128)(2,1)S(1)}, u32[]{:S(2)}, u32[]{:S(2)}) collective-permute-start(bf16[8,32,1024]{2,1,0:T(8,128)(2,1)S(1)} %constant_dynamic-update-slice_fusion.2.rest_10_), channel_id=1, source_target_pairs={{0,8},{8,0},{16,24},{24,16},{32,40},{40,32},{48,56},{56,48},{64,72... | collective-permute-start | bytes 1572872 | tf_op jit(solution)/shard_map/ppermute | solution.py:243
